TPU v7x, 128 devices: a whole 4x4x4 slice. The times are simulated.
128 devices in a mesh: gx: 16 (over x, y_hi, core), gy: 8 (over z, y_lo).
Axes of the slice: x: 4, y: 4 (y_hi: 2, y_lo: 2; y = y_hi * 2 + y_lo), z: 4, core: 2. Of those that a mesh axis runs over, the one named last changes fastest.
Arguments:
- fields: float32 [14, 48, 256, 1024], P(None, None, 'gx', 'gy'), may hold values from -1.5 to 9, as said below
- register: float32 [14, 48, 256, 1024], P(None, None, 'gx', 'gy'), may hold values from -0.15 to 0.15
Outputs:
- fields_next: float32 [14, 48, 256, 1024], P(None, None, 'gx', 'gy')
- register_next: float32 [14, 48, 256, 1024], P(None, None, 'gx', 'gy')
- flame_metrics: bfloat16 [5, 48, 256, 1024], P(None, 'gy', 'gx')
Inputs may be any that keep to these rules, and one draw needn't show every extreme that they name: fields[0] lies in 0.5 to 1.5; velocities fields[1:4] / fields[0] lie within -1 to 1; fields[4] / fields[0] minus half the squared speed lies in 1 to 4; each species density over fields[0] lies in 0.01 to 0.7.
All inputs are finite; a program needn't handle non-finite values.
Results may differ from a plain program's by a relative error of at most 0.0014.
The roundings to bfloat16 on the way count: a program that leaves them out, or rounds other values in their place, can miss the bound.
Values may be sent and summed in bfloat16 or wider, within the bound.
A program may use at most 192 MiB of HBM per device.

v0:
```python
import jax
import jax.numpy as jnp
import numpy as np
from jax import lax
from jax.sharding import PartitionSpec as P

GAMMA_LESS = 0.4
UNIVERSAL_R = 0.25
TIME_STEP = 0.25
SECTION_DECAY = -0.4178904745
SECTION_WEIGHT = 0.3792103129
GRAD_FLOOR = 0.1
PROGRESS_SCALE = 4.0
CENTRAL_WEIGHTS = (0.8, -0.2, 4.0 / 105.0, -1.0 / 280.0)
MOLAR_MASS = (2.0, 32.0, 16.0, 17.0, 18.0, 1.0, 33.0, 34.0, 28.0)
FORMATION_HEAT = (0.0, 0.0, 2.0, 0.3, -1.5, 3.0, 0.1, -0.4, 0.0)
ARRHENIUS_LIST = (
    (5, 1, (2, 3), 40.0, 2.0),
    (2, 0, (5, 3), 30.0, 1.2),
    (3, 0, (5, 4), 25.0, 0.8),
    (2, 4, (3, 3), 10.0, 1.6),
    (5, 1, (6,), 15.0, 0.2),
    (6, 5, (3, 3), 20.0, 0.3),
    (6, 6, (7, 1), 12.0, 0.4),
    (7, 8, (3, 3, 8), 8.0, 1.8),
)


def with_halo(block, sides, width):
    for axis, dim in sides:
        count = lax.axis_size(axis)
        forward = [(i, i + 1) for i in range(count - 1)]
        forward.append((count - 1, 0))
        backward = [(target, source) for source, target in forward]
        low = lax.ppermute(
            lax.slice_in_dim(block, block.shape[dim] - width, None, axis=dim), axis, forward
        )
        high = lax.ppermute(lax.slice_in_dim(block, 0, width, axis=dim), axis, backward)
        block = jnp.concatenate([low, block, high], axis=dim)
    return block


def make_table():
    table = np.zeros((14, 8))
    for column, kinetic_step_record in enumerate(ARRHENIUS_LIST):
        change = np.zeros(9)
        change[kinetic_step_record[0]] -= 1.0
        change[kinetic_step_record[1]] -= 1.0
        for product in kinetic_step_record[2]:
            change[product] += 1.0
        for species in range(9):
            mass_change = MOLAR_MASS[species] / 18.0 * change[species]
            table[5 + species, column] = mass_change
            table[4, column] -= FORMATION_HEAT[species] * mass_change
    return table


def inverse_weights():
    return np.array([18.0 / value for value in MOLAR_MASS])


def primitives(fields):
    velocity = fields[1:4] / fields[0]
    static_stress = GAMMA_LESS * (
        fields[4]
        - 0.5 * (fields[1] * velocity[0] + fields[2] * velocity[1] + fields[3] * velocity[2])
    )
    return (velocity, static_stress)


def reaction_rates(fields, static_stress):
    species_quantities = fields[5:14] * jnp.asarray(inverse_weights(), jnp.float32).reshape(
        9, 1, 1, 1
    )
    summed_quantity = jnp.sum(species_quantities, axis=0)
    cell_thermal_state = static_stress / (UNIVERSAL_R * summed_quantity)
    return jnp.stack(
        [
            kinetic_step_record[3]
            * jnp.exp(-kinetic_step_record[4] / cell_thermal_state)
            * species_quantities[kinetic_step_record[0]]
            * species_quantities[kinetic_step_record[1]]
            for kinetic_step_record in ARRHENIUS_LIST
        ]
    )


def directed_flux(fields, velocity, static_stress, direction):
    speed = velocity[direction]
    base = fields * speed
    select = jnp.asarray(np.eye(3)[direction].reshape(3, 1, 1, 1), jnp.float32)
    moment = base[1:4] + static_stress * select
    energy = base[4:5] + (static_stress * speed)[None]
    return jnp.concatenate([base[0:1], moment, energy, base[5:]], axis=0)


def rim_flux(piece, direction):
    velocity, static_stress = primitives(piece)
    return directed_flux(piece, velocity, static_stress, direction)


def central(extended, along, count):
    total = jnp.zeros(extended.shape[:along] + (count,) + extended.shape[along + 1 :], jnp.float32)
    for offset, weight in enumerate(CENTRAL_WEIGHTS, 1):
        ahead = lax.slice_in_dim(extended, 4 + offset, 4 + offset + count, axis=along)
        behind = lax.slice_in_dim(extended, 4 - offset, 4 - offset + count, axis=along)
        total = total + weight * (ahead - behind)
    return total


def flame_metrics(padded):
    scalar = padded[0]
    grad_z = (scalar[2:, 1:-1, 1:-1] - scalar[:-2, 1:-1, 1:-1]) * 0.5
    grad_x = (scalar[1:-1, 2:, 1:-1] - scalar[1:-1, :-2, 1:-1]) * 0.5
    grad_y = (scalar[1:-1, 1:-1, 2:] - scalar[1:-1, 1:-1, :-2]) * 0.5
    magnitude = jnp.maximum(
        jnp.sqrt(grad_x * grad_x + grad_y * grad_y + grad_z * grad_z), GRAD_FLOOR
    )
    normal_x = -grad_x / magnitude
    normal_y = -grad_y / magnitude
    normal_z = -grad_z / magnitude
    curvature = 0.5 * (normal_x[1:-1, 2:, 1:-1] - normal_x[1:-1, :-2, 1:-1])
    curvature = curvature + 0.5 * (normal_y[1:-1, 1:-1, 2:] - normal_y[1:-1, 1:-1, :-2])
    curvature = curvature + 0.5 * (normal_z[2:, 1:-1, 1:-1] - normal_z[:-2, 1:-1, 1:-1])
    inner = (normal_x[1:-1, 1:-1, 1:-1], normal_y[1:-1, 1:-1, 1:-1], normal_z[1:-1, 1:-1, 1:-1])
    speeds = padded[1:4]
    gradients = []
    for component in range(3):
        piece = speeds[component]
        along_x = (piece[2:-2, 3:-1, 2:-2] - piece[2:-2, 1:-3, 2:-2]) * 0.5
        along_y = (piece[2:-2, 2:-2, 3:-1] - piece[2:-2, 2:-2, 1:-3]) * 0.5
        along_z = (piece[3:-1, 2:-2, 2:-2] - piece[1:-3, 2:-2, 2:-2]) * 0.5
        gradients.append((along_x, along_y, along_z))
    strain = gradients[0][0] + gradients[1][1] + gradients[2][2]
    for component in range(3):
        for direction in range(3):
            strain = strain - inner[component] * inner[direction] * gradients[component][direction]
    return jnp.stack([inner[0], inner[1], inner[2], curvature, strain])


def per_device(fields, register):
    count_z = fields.shape[1]
    count_x = fields.shape[2]
    count_y = fields.shape[3]
    velocity, static_stress = primitives(fields)
    probe = jnp.concatenate(
        [(PROGRESS_SCALE * (fields[9] / fields[0]))[None], velocity], axis=0
    ).astype(jnp.bfloat16)
    bricks = lax.all_to_all(probe, "gy", split_axis=1, concat_axis=3, tiled=True)
    rimmed = with_halo(bricks, (("gx", 2), ("gy", 1)), 2)
    padded = jnp.concatenate([rimmed[:, :, :, -2:], rimmed, rimmed[:, :, :, :2]], axis=3)
    metrics = flame_metrics(padded.astype(jnp.float32)).astype(jnp.bfloat16)
    flux_x = directed_flux(fields, velocity, static_stress, 0)
    flux_y = directed_flux(fields, velocity, static_stress, 1)
    flux_z = directed_flux(fields, velocity, static_stress, 2)
    rates = reaction_rates(fields, static_stress)
    source = jnp.tensordot(
        jnp.asarray(make_table(), jnp.float32), rates, axes=1, precision=lax.Precision.HIGHEST
    )
    haloed = with_halo(fields, (("gx", 2), ("gy", 3)), 4)
    lower_x = rim_flux(haloed[:, :, :4, 4 : 4 + count_y], 0)
    upper_x = rim_flux(haloed[:, :, 4 + count_x :, 4 : 4 + count_y], 0)
    lower_y = rim_flux(haloed[:, :, 4 : 4 + count_x, :4], 1)
    upper_y = rim_flux(haloed[:, :, 4 : 4 + count_x, 4 + count_y :], 1)
    extended_x = jnp.concatenate([lower_x, flux_x, upper_x], axis=2)
    extended_y = jnp.concatenate([lower_y, flux_y, upper_y], axis=3)
    extended_z = jnp.concatenate([flux_z[:, -4:], flux_z, flux_z[:, :4]], axis=1)
    advection = (
        central(extended_x, 2, count_x)
        + central(extended_y, 3, count_y)
        + central(extended_z, 1, count_z)
    )
    register_next = SECTION_DECAY * register + TIME_STEP * (source - advection)
    fields_next = fields + SECTION_WEIGHT * register_next
    return (fields_next, register_next, metrics)


def solution(mesh):
    in_specs = (P(None, None, "gx", "gy"), P(None, None, "gx", "gy"))
    out_specs = (P(None, None, "gx", "gy"), P(None, None, "gx", "gy"), P(None, "gy", "gx", None))
    return jax.shard_map(
        per_device, mesh=mesh, in_specs=in_specs, out_specs=out_specs, check_vma=False
    )
```

profile of v0, /device:TPU:1, one launch (start us, length us, event | category | flops | bytes accessed | tf_op | source)
XLA Modules:
  0.0 273.7 jit_solution(11552712074932553879)
XLA Ops:
  0.7 3.3 %fusion.129 = (f32[14,48,4,128]{3,2,1,0:T(4,128)S(1)}, f32[14,48,4,128]{3,2,1,0:T(4,128)S(1)}) fusion(f32[14,48,16,128]{3,2,1,0:T(8,128)} %param.11), kind=kLoop, calls=%fused_computation.251 | loop fusion | bytes 5505024 | tf_op jit(solution)/shard_map/slice | solution.py:36
  4.0 1.2 copy.259
  5.2 1.4 collective-permute-start
  6.6 1.2 copy.260
  7.9 2.9 %collective-permute-start.1 = (f32[14,48,4,128]{3,1,2,0:T(8,128)}, f32[14,48,4,128]{3,1,2,0:T(8,128)}, u32[]{:S(2)}, u32[]{:S(2)}) collective-permute-start(f32[14,48,4,128]{3,1,2,0:T(8,128)} %copy.260), channel_id=1, source_target_pairs={{0,8},{8,16},{16,24},{24,32},{32,40},{40,48},{48,56},{56,64},{64,7... | collective-permute-start | bytes 4128776 | tf_op jit(solution)/shard_map/ppermute | solution.py:35
  10.8 0.5 fusion.121
  11.5 1.6 fusion.94
  13.2 1.1 copy.256
  14.3 5.8 %all-to-all-start = ((bf16[4,48,16,128]{3,2,0,1:T(8,128)(2,1)}), bf16[4,48,16,128]{3,2,0,1:T(8,128)(2,1)}, u32[]{:S(2)}, u32[]{:S(2)}) async-start(bf16[4,48,16,128]{3,2,0,1:T(8,128)(2,1)} %copy.256), calls=%async_computation | async-start | bytes 1572864 | tf_op jit(solution)/shard_map/all_to_all | solution.py:149
  20.1 8.4 %broadcast_multiply_fusion.2 = (f32[14,48,16,128]{3,2,1,0:T(8,128)S(1)}, f32[14,48,16,128]{3,2,1,0:T(8,128)}, f32[14,48,16,128]{3,2,1,0:T(8,128)}) fusion(f32[14,48,16,128]{3,2,1,0:T(8,128)} %param.11, f32[48,16,128]{2,1,0:T(8,128)S(1)} %get-tuple-element.63, f32[48,16,128]{2,1,0:T(8,128)S(1)} %get-tuple-element.65, f32[48,16,128]{2,1,0:T(8,128)S(1)} %get-tuple-element.64), kind=kLoop, calls=%fused_computation.56 | loop fusion | flops 4128768 | bytes 23199744 | tf_op jit(solution)/shard_map/mul | solution.py:90
  28.5 6.1 %slice.784 = f32[9,48,16,128]{3,2,1,0:T(8,128)} slice(f32[14,48,16,128]{3,2,1,0:T(8,128)} %get-tuple-element.41), slice={[5:14], [0:48], [0:16], [0:128]} | slice | bytes 7077888 | tf_op jit(solution)/shard_map/slice | solution.py:94
  34.6 1.2 copy-done.13
  36.4 1.1 fusion.128
  37.5 2.1 fusion.130
  39.6 2.2 fusion.131
  41.8 1.8 copy-done.14
  43.5 3.6 %slice_add_fusion.2 = (f32[3,48,16,128]{3,2,1,0:T(8,128)}, f32[3,48,16,128]{3,2,1,0:T(8,128)}, f32[3,48,16,128]{3,2,1,0:T(8,128)}) fusion(f32[14,48,16,128]{3,2,1,0:T(8,128)S(1)} %get-tuple-element.40, f32[3]{0:T(128)S(1)} %copy-done.26, f32[48,16,128]{2,1,0:T(8,128)S(1)} %bitcast.144, f32[3]{0:T(128)S(1)} %copy-done.27, ...), kind=kLoop, calls=%fused_computation.60 | loop fusion | flops 1769472 | bytes 7471140 | tf_op jit(solution)/shard_map/add | solution.py:92
  47.1 6.4 %all-to-all-done = bf16[4,48,16,128]{3,2,0,1:T(8,128)(2,1)} async-done(((bf16[4,48,16,128]{3,2,0,1:T(8,128)(2,1)}), bf16[4,48,16,128]{3,2,0,1:T(8,128)(2,1)}, u32[]{:S(2)}, u32[]{:S(2)}) %all-to-all-start) | async-done | bytes 786464 | tf_op jit(solution)/shard_map/all_to_all | solution.py:149
  53.5 2.5 copy.257
  56.0 2.1 all_to_all.16
  58.2 1.9 fusion.133
  60.1 3.2 %collective-permute-start.4 = (bf16[4,6,2,1024]{3,2,1,0:T(2,128)(2,1)}, bf16[4,6,2,1024]{3,2,1,0:T(2,128)(2,1)}, u32[]{:S(2)}, u32[]{:S(2)}) collective-permute-start(bf16[4,6,2,1024]{3,2,1,0:T(2,128)(2,1)} %get-tuple-element.68), channel_id=1, source_target_pairs={{0,8},{8,16},{16,24},{24,32},{32,40},{40,48},{48,56},{56,64},{64,7... | collective-permute-start | bytes 294920 | tf_op jit(solution)/shard_map/ppermute | solution.py:35
  63.4 6.7 %fusion.1 = (f32[14,52,16,128]{3,2,1,0:T(8,128)}, f32[14,52,16,128]{3,2,1,0:T(8,128)}) fusion(f32[9,48,16,128]{3,2,1,0:T(8,128)S(1)} %copy-done.5, f32[1,48,16,128]{3,2,1,0:T(8,128)} %get-tuple-element.52, f32[3,48,16,128]{3,2,1,0:T(8,128)} %get-tuple-element.77, f32[1,48,16,128]{3,2,1,0:T(8,128)} %get-tuple-element.51), kind=kLoop, calls=%fused_computation.9 | loop fusion | flops 20873216 | bytes 17432576 | tf_op jit(solution)/shard_map/concatenate | solution.py:167
  70.1 11.2 %copy.251 = f32[14,48,16,128]{1,2,3,0:T(8,128)} copy(f32[14,48,16,128]{3,2,1,0:T(8,128)} %param.11) | data formatting | bytes 11010048 | tf_op args[0]
  81.3 2.4 slice.744
  83.8 4.1 %slice.706 = f32[9,48,16,128]{3,2,1,0:T(8,128)} slice(f32[14,48,16,128]{3,2,1,0:T(8,128)} %copy-done.3), slice={[5:14], [0:48], [0:16], [0:128]} | slice | bytes 7077888 | tf_op jit(solution)/shard_map/slice | solution.py:94
  87.9 1.2 pad_maximum_fusion.16
  89.1 1.1 collective-permute-start.7
  90.3 0.4 collective-permute-start.6
  90.7 7.7 %fusion.28 = f32[14,48,16,128]{3,0,2,1:T(8,128)} fusion(f32[14,8,1,1]{0,1,3,2:T(8,128)S(1)} %copy-done.25, f32[8,48,16,128]{3,2,1,0:T(8,128)S(1)} %copy-done.15), kind=kOutput, calls=%fused_computation.52 | convolution fusion | flops 132120576 | bytes 8651200 | tf_op jit(solution)/shard_map/dot_general | solution.py:157
  98.4 1.7 collective-permute-done.7
  100.1 7.7 %collective-permute-done.6 = bf16[4,2,20,1024]{3,2,1,0:T(8,128)(2,1)S(1)} collective-permute-done((bf16[4,2,20,1024]{3,2,1,0:T(8,128)(2,1)S(1)}, bf16[4,2,20,1024]{3,2,1,0:T(8,128)(2,1)S(1)}, u32[]{:S(2)}, u32[]{:S(2)}) %collective-permute-start.6) | collective-permute-done | bytes 327712 | tf_op jit(solution)/shard_map/ppermute | solution.py:35
  107.8 1.6 pad_maximum_fusion.7
  109.4 1.3 copy-done.6
  110.7 0.9 fusion.132
  111.6 5.3 %concatenate.93 = bf16[4,10,20,1028]{3,2,1,0:T(8,128)(2,1)} concatenate(bf16[4,10,20,2]{3,2,1,0:T(8,128)(2,1)} %get-tuple-element.60, bf16[4,10,20,1024]{3,2,1,0:T(8,128)(2,1)} %copy-done.6, bf16[4,10,20,2]{3,2,1,0:T(8,128)(2,1)} %get-tuple-element.59), dimensions={3} | concatenate | bytes 3289600 | tf_op jit(solution)/shard_map/concatenate | solution.py:151
  116.9 1.9 convert_element_type.2
  118.8 0.3 slice_bitcast_fusion.2
  119.1 1.3 negate_divide_fusion
  120.3 0.8 negate_divide_fusion.1
  121.6 0.6 bitcast_dynamic-update-slice_fusion.1
  122.2 2.4 bitcast_dynamic-update-slice_fusion
  124.6 1.0 slice_bitcast_fusion.9
  125.7 1.9 copy.237
  127.7 1.9 broadcast_multiply_fusion.4
  129.6 1.0 slice_add_fusion.11
  130.6 0.9 slice_bitcast_fusion.8
  131.5 1.9 copy.245
  133.5 1.9 broadcast_multiply_fusion.3
  135.4 0.9 slice_add_fusion.10
  136.3 0.2 copy-done.10
  136.5 4.1 %copy.252 = f32[14,48,4,128]{1,2,3,0:T(4,128)} copy(f32[14,48,4,128]{3,1,2,0:T(8,128)} %collective-permute-done) | data formatting | bytes 2752512 | tf_op jit(solution)/shard_map/ppermute | solution.py:38
  140.6 4.1 %copy.250 = f32[14,48,4,128]{1,2,3,0:T(4,128)} copy(f32[14,48,4,128]{3,1,2,0:T(8,128)} %collective-permute-done.1) | data formatting | bytes 2752512 | tf_op jit(solution)/shard_map/ppermute | solution.py:35
  144.8 1.8 pad_maximum_fusion.11
  146.6 1.3 collective-permute-start.2
  147.9 0.6 collective-permute-start.3
  149.1 6.9 %maximum_maximum_fusion.1 = (f32[14,48,20,128]{3,2,1,0:T(8,128)}, f32[14,48,20,128]{3,2,1,0:T(8,128)}) fusion(f32[9,48,4,128]{3,2,1,0:T(4,128)S(1)} %slice-done, f32[1,48,4,128]{3,2,1,0:T(4,128)S(1)} %copy-done.18, f32[3,48,4,128]{3,2,1,0:T(4,128)S(1)} %get-tuple-element.78, f32[1,48,4,128]{3,2,1,0:T(4,128)S(1)} %copy-done.19, ...), kind=kLoop, calls=%fused_computation.2 | loop fusion | flops 24084480 | bytes 22020096 | tf_op jit(solution)/shard_map/concatenate | solution.py:165
  156.0 7.1 %collective-permute-done.2 = f32[14,48,24,4]{1,2,3,0:T(8,128)S(1)} collective-permute-done((f32[14,48,24,4]{1,2,3,0:T(8,128)S(1)}, f32[14,48,24,4]{1,2,3,0:T(8,128)S(1)}, u32[]{:S(2)}, u32[]{:S(2)}) %collective-permute-start.2) | collective-permute-done | bytes 258080 | tf_op jit(solution)/shard_map/ppermute | solution.py:38
  163.2 13.4 %collective-permute-done.3 = f32[14,48,24,4]{1,2,3,0:T(8,128)S(1)} collective-permute-done((f32[14,48,24,4]{1,2,3,0:T(8,128)S(1)}, f32[14,48,24,4]{1,2,3,0:T(8,128)S(1)}, u32[]{:S(2)}, u32[]{:S(2)}) %collective-permute-start.3) | collective-permute-done | bytes 258080 | tf_op jit(solution)/shard_map/ppermute | solution.py:35
  176.9 1.0 pad_maximum_fusion.12
  178.0 4.6 %copy.253 = f32[14,48,16,4]{3,2,1,0:T(8,128)} copy(f32[14,48,16,4]{1,2,3,0:T(8,128)} %get-tuple-element.82) | data formatting | bytes 344064 | tf_op jit(solution)/shard_map/concatenate | solution.py:94
  182.6 4.6 %copy.254 = f32[14,48,16,4]{3,2,1,0:T(8,128)} copy(f32[14,48,16,4]{1,2,3,0:T(8,128)} %get-tuple-element.83) | data formatting | bytes 344064 | tf_op jit(solution)/shard_map/concatenate | solution.py:94
  187.2 15.8 %pad_maximum_fusion = (f32[14,48,16,132]{3,2,1,0:T(8,128)}, f32[14,48,16,132]{3,2,1,0:T(8,128)}) fusion(f32[14,48,16,4]{3,2,1,0:T(8,128)} %copy.253, f32[9,48,16,128]{3,2,1,0:T(8,128)S(1)} %slice.744, f32[1,48,16,128]{3,2,1,0:T(8,128)} %get-tuple-element.48, f32[3,48,16,128]{3,2,1,0:T(8,128)} %get-tuple-element.76, f32[1,48,16,128]{3,2,1,0:T(8,128)} %get-tuple-element.47, ...), kind=kLoop, calls=%fused_computation | loop fusion | flops 11354112 | bytes 17203200 | tf_op jit(solution)/shard_map/concatenate | solution.py:166
  203.1 70.5 %multiply_add_fusion = (f32[14,48,16,128]{3,2,1,0:T(8,128)}, f32[14,48,16,128]{3,2,1,0:T(8,128)}) fusion(f32[14,48,16,128]{3,2,1,0:T(8,128)} %param.11, f32[14,52,16,128]{3,2,1,0:T(8,128)} %get-tuple-element.50, f32[14,52,16,128]{3,2,1,0:T(8,128)} %get-tuple-element.49, f32[14,48,16,132]{3,2,1,0:T(8,128)} %get-tuple-element.44, ...), kind=kLoop, calls=%fused_computation.50 | loop fusion | flops 56426496 | bytes 159645696 | tf_op jit(solution)/shard_map/add | solution.py:174
  (95 shorter events, 2.4 us)
Async XLA Ops:
  0.6 10.2 %copy-start.29 = (f32[9]{0:T(128)S(1)}, f32[9]{0:T(128)}, u32[]{:S(2)}) copy-start(f32[9]{0:T(128)} %constant.27.clone) | copy-start | bytes 112
  0.6 10.1 %copy-start = (f32[14,48,16,128]{3,2,1,0:T(8,128)S(1)}, f32[14,48,16,128]{3,2,1,0:T(8,128)}, u32[]{:S(2)}) copy-start(f32[14,48,16,128]{3,2,1,0:T(8,128)} %param.11) | copy-start | bytes 16515076
  5.2 119.4 %collective-permute-start = (f32[14,48,4,128]{3,1,2,0:T(8,128)}, f32[14,48,4,128]{3,1,2,0:T(8,128)}, u32[]{:S(2)}, u32[]{:S(2)}) collective-permute-start(f32[14,48,4,128]{3,1,2,0:T(8,128)} %copy.259), channel_id=1, source_target_pairs={{8,0},{16,8},{24,16},{32,24},{40,32},{48,40},{56,48},{64,56},{72,6... | collective-permute-start | bytes 4128776 | tf_op jit(solution)/shard_map/ppermute | solution.py:38
  7.9 122.7 %collective-permute-start.1 = (f32[14,48,4,128]{3,1,2,0:T(8,128)}, f32[14,48,4,128]{3,1,2,0:T(8,128)}, u32[]{:S(2)}, u32[]{:S(2)}) collective-permute-start(f32[14,48,4,128]{3,1,2,0:T(8,128)} %copy.260), channel_id=1, source_target_pairs={{0,8},{8,16},{16,24},{24,32},{32,40},{40,48},{48,56},{56,64},{64,7... | collective-permute-start | bytes 4128776 | tf_op jit(solution)/shard_map/ppermute | solution.py:35
  11.3 1.9 copy-start.1
  14.3 39.2 %all-to-all-start = ((bf16[4,48,16,128]{3,2,0,1:T(8,128)(2,1)}), bf16[4,48,16,128]{3,2,0,1:T(8,128)(2,1)}, u32[]{:S(2)}, u32[]{:S(2)}) async-start(bf16[4,48,16,128]{3,2,0,1:T(8,128)(2,1)} %copy.256), calls=%async_computation | async-start | bytes 1572864 | tf_op jit(solution)/shard_map/all_to_all | solution.py:149
  28.5 13.3 %copy-start.3 = (f32[14,48,16,128]{3,2,1,0:T(8,128)}, f32[14,48,16,128]{3,2,1,0:T(8,128)S(1)}, u32[]{:S(2)}) copy-start(f32[14,48,16,128]{3,2,1,0:T(8,128)S(1)} %get-tuple-element.40) | copy-start | bytes 16515076
  28.5 6.1 %copy-start.2 = (f32[9,48,16,128]{3,2,1,0:T(8,128)S(1)}, f32[9,48,16,128]{3,2,1,0:T(8,128)}, u32[]{:S(2)}) copy-start(f32[9,48,16,128]{3,2,1,0:T(8,128)} %copy-done.1) | copy-start | bytes 10616836
  28.5 7.3 %copy-start.13 = (f32[8,48,16,128]{3,2,1,0:T(8,128)S(1)}, f32[8,48,16,128]{3,2,1,0:T(8,128)}, u32[]{:S(2)}) copy-start(f32[8,48,16,128]{3,2,1,0:T(8,128)} %get-tuple-element.21) | copy-start | bytes 9437188
  36.3 7.2 %copy-start.26 = (f32[3]{0:T(128)S(1)}, f32[3]{0:T(128)}, u32[]{:S(2)}) copy-start(f32[3]{0:T(128)} %constant.29) | copy-start | bytes 40
  36.3 7.2 %copy-start.27 = (f32[3]{0:T(128)S(1)}, f32[3]{0:T(128)}, u32[]{:S(2)}) copy-start(f32[3]{0:T(128)} %constant.30) | copy-start | bytes 40
  36.4 7.2 %copy-start.28 = (f32[3]{0:T(128)S(1)}, f32[3]{0:T(128)}, u32[]{:S(2)}) copy-start(f32[3]{0:T(128)} %constant.31) | copy-start | bytes 40
  41.8 1.8 copy-start.14
  47.1 16.2 %copy-start.5 = (f32[9,48,16,128]{3,2,1,0:T(8,128)S(1)}, f32[9,48,16,128]{3,2,1,0:T(8,128)}, u32[]{:S(2)}) copy-start(f32[9,48,16,128]{3,2,1,0:T(8,128)} %slice.784) | copy-start | bytes 10616836
  60.1 27.8 %collective-permute-start.5 = (bf16[4,6,2,1024]{3,2,1,0:T(2,128)(2,1)}, bf16[4,6,2,1024]{3,2,1,0:T(2,128)(2,1)}, u32[]{:S(2)}, u32[]{:S(2)}) collective-permute-start(bf16[4,6,2,1024]{3,2,1,0:T(2,128)(2,1)} %get-tuple-element.69), channel_id=1, source_target_pairs={{8,0},{16,8},{24,16},{32,24},{40,32},{48,40},{56,48},{64,56},{72,6... | collective-permute-start | bytes 294920 | tf_op jit(solution)/shard_map/ppermute | solution.py:38
  60.1 27.8 %collective-permute-start.4 = (bf16[4,6,2,1024]{3,2,1,0:T(2,128)(2,1)}, bf16[4,6,2,1024]{3,2,1,0:T(2,128)(2,1)}, u32[]{:S(2)}, u32[]{:S(2)}) collective-permute-start(bf16[4,6,2,1024]{3,2,1,0:T(2,128)(2,1)} %get-tuple-element.68), channel_id=1, source_target_pairs={{0,8},{8,16},{16,24},{24,32},{32,40},{40,48},{48,56},{56,64},{64,7... | collective-permute-start | bytes 294920 | tf_op jit(solution)/shard_map/ppermute | solution.py:35
  81.3 6.6 %copy-start.7 = (bf16[4,6,16,1024]{3,2,1,0:T(8,128)(2,1)S(1)}, bf16[4,6,16,1024]{3,2,1,0:T(8,128)(2,1)}, u32[]{:S(2)}) copy-start(bf16[4,6,16,1024]{3,2,1,0:T(8,128)(2,1)} %all_to_all.16) | copy-start | bytes 2359300
  83.7 6.9 %copy-start.15 = (f32[8,48,16,128]{3,2,1,0:T(8,128)S(1)}, f32[8,48,16,128]{3,2,1,0:T(8,128)}, u32[]{:S(2)}) copy-start(f32[8,48,16,128]{3,2,1,0:T(8,128)} %copy-done.14) | copy-start | bytes 9437188
  83.7 6.9 %copy-start.25 = (f32[14,8,1,1]{0,1,3,2:T(8,128)S(1)}, f32[14,8,1,1]{0,1,3,2:T(8,128)}, u32[]{:S(2)}) copy-start(f32[14,8,1,1]{0,1,3,2:T(8,128)} %constant.80) | copy-start | bytes 1348
  89.1 11.0 %collective-permute-start.7 = (bf16[4,2,20,1024]{3,2,1,0:T(8,128)(2,1)S(1)}, bf16[4,2,20,1024]{3,2,1,0:T(8,128)(2,1)S(1)}, u32[]{:S(2)}, u32[]{:S(2)}) collective-permute-start(bf16[4,2,20,1024]{3,2,1,0:T(8,128)(2,1)S(1)} %get-tuple-element.67), channel_id=1, source_target_pairs={{1,0},{2,1},{3,2},{4,3},{5,4},{6,5},{7,6},{0,7},{9,8},{10,9},{11,1... | collective-permute-start | bytes 983048 | tf_op jit(solution)/shard_map/ppermute | solution.py:38
  90.3 17.6 %collective-permute-start.6 = (bf16[4,2,20,1024]{3,2,1,0:T(8,128)(2,1)S(1)}, bf16[4,2,20,1024]{3,2,1,0:T(8,128)(2,1)S(1)}, u32[]{:S(2)}, u32[]{:S(2)}) collective-permute-start(bf16[4,2,20,1024]{3,2,1,0:T(8,128)(2,1)S(1)} %get-tuple-element.66), channel_id=1, source_target_pairs={{0,1},{1,2},{2,3},{3,4},{4,5},{5,6},{6,7},{7,0},{8,9},{9,10},{10,1... | collective-permute-start | bytes 983048 | tf_op jit(solution)/shard_map/ppermute | solution.py:35
  109.4 1.3 copy-start.6
  124.6 8.8 %copy-start.24 = (bf16[5,6,16,1024]{3,2,1,0:T(8,128)(2,1)}, bf16[5,6,16,1024]{3,2,1,0:T(8,128)(2,1)S(1)}, u32[]{:S(2)}) copy-start(bf16[5,6,16,1024]{3,2,1,0:T(8,128)(2,1)S(1)} %bitcast_dynamic-update-slice_fusion) | copy-start | bytes 2949124
  129.6 6.8 %copy-start.8 = (f32[14,48,4,128]{3,2,1,0:T(4,128)}, f32[14,48,4,128]{3,2,1,0:T(4,128)S(1)}, u32[]{:S(2)}) copy-start(f32[14,48,4,128]{3,2,1,0:T(4,128)S(1)} %broadcast_multiply_fusion.4) | copy-start | bytes 4128772
  135.4 1.2 copy-start.10
  144.7 3.8 %copy-start.9 = (f32[14,48,4,128]{3,2,1,0:T(4,128)S(1)}, f32[14,48,4,128]{3,2,1,0:T(4,128)}, u32[]{:S(2)}) copy-start(f32[14,48,4,128]{3,2,1,0:T(4,128)} %copy-done.8) | copy-start | bytes 4128772
  144.7 3.8 %copy-start.11 = (f32[14,48,4,128]{3,2,1,0:T(4,128)S(1)}, f32[14,48,4,128]{3,2,1,0:T(4,128)}, u32[]{:S(2)}) copy-start(f32[14,48,4,128]{3,2,1,0:T(4,128)} %copy-done.10) | copy-start | bytes 4128772
  144.7 3.8 %copy-start.22 = (f32[1,48,4,128]{3,2,1,0:T(4,128)S(1)}, f32[1,48,4,128]{3,2,1,0:T(4,128)}, u32[]{:S(2)}) copy-start(f32[1,48,4,128]{3,2,1,0:T(4,128)} %get-tuple-element.24) | copy-start | bytes 294916
  144.7 3.8 %copy-start.23 = (f32[1,48,4,128]{3,2,1,0:T(4,128)S(1)}, f32[1,48,4,128]{3,2,1,0:T(4,128)}, u32[]{:S(2)}) copy-start(f32[1,48,4,128]{3,2,1,0:T(4,128)} %get-tuple-element.26) | copy-start | bytes 294916
  144.7 4.0 %copy-start.4 = (f32[9,48,16,128]{3,2,1,0:T(8,128)S(1)}, f32[9,48,16,128]{3,2,1,0:T(8,128)}, u32[]{:S(2)}) copy-start(f32[9,48,16,128]{3,2,1,0:T(8,128)} %slice.706) | copy-start | bytes 10616836
  144.7 4.0 %slice-start = ((f32[14,48,4,128]{3,2,1,0:T(4,128)}), f32[9,48,4,128]{3,2,1,0:T(4,128)S(1)}, s32[]{:S(2)}) async-start(f32[14,48,4,128]{3,2,1,0:T(4,128)} %copy-done.8), calls=%async_computation.1 | async-start | bytes 1769472 | tf_op jit(solution)/shard_map/slice | solution.py:94
  144.7 4.0 %slice-start.1 = ((f32[14,48,4,128]{3,2,1,0:T(4,128)}), f32[9,48,4,128]{3,2,1,0:T(4,128)S(1)}, s32[]{:S(2)}) async-start(f32[14,48,4,128]{3,2,1,0:T(4,128)} %copy-done.10), calls=%async_computation.2 | async-start | bytes 1769472 | tf_op jit(solution)/shard_map/slice | solution.py:94
  144.7 4.1 %copy-start.12 = (f32[3,48,16,128]{3,2,1,0:T(8,128)S(1)}, f32[3,48,16,128]{3,2,1,0:T(8,128)}, u32[]{:S(2)}) copy-start(f32[3,48,16,128]{3,2,1,0:T(8,128)} %get-tuple-element.75) | copy-start | bytes 3538948
  144.8 4.1 %copy-start.16 = (f32[1,48,16,128]{3,2,1,0:T(8,128)S(1)}, f32[1,48,16,128]{3,2,1,0:T(8,128)}, u32[]{:S(2)}) copy-start(f32[1,48,16,128]{3,2,1,0:T(8,128)} %get-tuple-element.38) | copy-start | bytes 1179652
  144.8 4.2 %copy-start.17 = (f32[1,48,16,128]{3,2,1,0:T(8,128)S(1)}, f32[1,48,16,128]{3,2,1,0:T(8,128)}, u32[]{:S(2)}) copy-start(f32[1,48,16,128]{3,2,1,0:T(8,128)} %get-tuple-element.39) | copy-start | bytes 1179652
  144.8 4.2 %copy-start.18 = (f32[1,48,4,128]{3,2,1,0:T(4,128)S(1)}, f32[1,48,4,128]{3,2,1,0:T(4,128)}, u32[]{:S(2)}) copy-start(f32[1,48,4,128]{3,2,1,0:T(4,128)} %get-tuple-element.23) | copy-start | bytes 294916
  144.8 4.3 %copy-start.19 = (f32[1,48,4,128]{3,2,1,0:T(4,128)S(1)}, f32[1,48,4,128]{3,2,1,0:T(4,128)}, u32[]{:S(2)}) copy-start(f32[1,48,4,128]{3,2,1,0:T(4,128)} %get-tuple-element.61) | copy-start | bytes 294916
  144.8 4.3 %copy-start.20 = (f32[1,48,4,128]{3,2,1,0:T(4,128)S(1)}, f32[1,48,4,128]{3,2,1,0:T(4,128)}, u32[]{:S(2)}) copy-start(f32[1,48,4,128]{3,2,1,0:T(4,128)} %get-tuple-element.25) | copy-start | bytes 294916
  144.8 4.3 %copy-start.21 = (f32[1,48,4,128]{3,2,1,0:T(4,128)S(1)}, f32[1,48,4,128]{3,2,1,0:T(4,128)}, u32[]{:S(2)}) copy-start(f32[1,48,4,128]{3,2,1,0:T(4,128)} %get-tuple-element.62) | copy-start | bytes 294916
  146.6 16.5 %collective-permute-start.2 = (f32[14,48,24,4]{1,2,3,0:T(8,128)S(1)}, f32[14,48,24,4]{1,2,3,0:T(8,128)S(1)}, u32[]{:S(2)}, u32[]{:S(2)}) collective-permute-start(f32[14,48,24,4]{1,2,3,0:T(8,128)S(1)} %get-tuple-element.31), channel_id=1, source_target_pairs={{1,0},{2,1},{3,2},{4,3},{5,4},{6,5},{7,6},{0,7},{9,8},{10,9},{11,1... | collective-permute-start | bytes 774152 | tf_op jit(solution)/shard_map/ppermute | solution.py:38
  147.9 28.8 %collective-permute-start.3 = (f32[14,48,24,4]{1,2,3,0:T(8,128)S(1)}, f32[14,48,24,4]{1,2,3,0:T(8,128)S(1)}, u32[]{:S(2)}, u32[]{:S(2)}) collective-permute-start(f32[14,48,24,4]{1,2,3,0:T(8,128)S(1)} %get-tuple-element.32), channel_id=1, source_target_pairs={{0,1},{1,2},{2,3},{3,4},{4,5},{5,6},{6,7},{7,0},{8,9},{9,10},{10,1... | collective-permute-start | bytes 774152 | tf_op jit(solution)/shard_map/ppermute | solution.py:35
where the time goes:
time: 276 us; the launch traced here: 274 us
  other arithmetic  139 us (50%)
  local copies, waits for them, and re-layouts  72.4 us (26%)
  waiting for transfers between devices  36.3 us (13%)
  starting transfers between devices  16.9 us (6%)
  matrix products  7.72 us (3%)
    add x1, other arithmetic, per_device(): fields_next = fields + SECTION_WEIGHT * register_next  70.5 us
    ppermute x4, waiting for transfers between devices, with_halo(): lax.ppermute(lax.slice_in_dim(block, block.shape[dim] - width, None, axis...  21.2 us
    unnamed x66, local copies, waits for them, and re-layouts  19 us
    concatenate x1, other arithmetic, per_device(): extended_y = jnp.concatenate([lower_y, flux_y, upper_y], axis=3)  15.8 us
    slice x9, local copies, waits for them, and re-layouts, directed_flux(): return jnp.concatenate([base[0:1], moment, energy, base[5:]], axis=0)  12.7 us
    mul x5, other arithmetic, directed_flux(): base = fields * speed  12.2 us
    concatenate x2, local copies, waits for them, and re-layouts, directed_flux(): return jnp.concatenate([base[0:1], moment, energy, base[5:]], axis=0)  9.24 us
    ppermute x4, waiting for transfers between devices, with_halo(): lax.ppermute(lax.slice_in_dim(block, 0, width, axis=dim), axis, backward)  8.78 us
  transfers between devices with their start and end apart: 9, of which 5 were waited for; matrix products, arithmetic and copies ran while one was open for 35% of the time, Pallas kernels for 0%

commit v1 on v0

v1 whole, which is shorter than its diff:
```python
import jax
import jax.numpy as jnp
import numpy as np
from jax import lax
from jax.experimental import pallas as pl
from jax.experimental.pallas import tpu as pltpu
from jax.sharding import PartitionSpec as P

MESH = pl.DeviceIdType.MESH
F32, BF16 = jnp.float32, jnp.bfloat16
DECAY = -0.4178904745
STEP = 0.25
WEIGHT = 0.3792103129
C = (0.8, -0.2, 4.0 / 105.0, -1.0 / 280.0)
MOLAR_MASS = (2.0, 32.0, 16.0, 17.0, 18.0, 1.0, 33.0, 34.0, 28.0)
FORMATION_HEAT = (0.0, 0.0, 2.0, 0.3, -1.5, 3.0, 0.1, -0.4, 0.0)
REACTIONS = (
    (5, 1, (2, 3), 40.0, 2.0),
    (2, 0, (5, 3), 30.0, 1.2),
    (3, 0, (5, 4), 25.0, 0.8),
    (2, 4, (3, 3), 10.0, 1.6),
    (5, 1, (6,), 15.0, 0.2),
    (6, 5, (3, 3), 20.0, 0.3),
    (6, 6, (7, 1), 12.0, 0.4),
    (7, 8, (3, 3, 8), 8.0, 1.8),
)
NF, NZ, CX, LY = 14, 48, 16, 128
ROWS = NZ * CX
HALF = ROWS // 2


def make_table():
    table = np.zeros((14, 8))
    for column, record in enumerate(REACTIONS):
        change = np.zeros(9)
        change[record[0]] -= 1.0
        change[record[1]] -= 1.0
        for product in record[2]:
            change[product] += 1.0
        for species in range(9):
            mass_change = MOLAR_MASS[species] / 18.0 * change[species]
            table[5 + species, column] = mass_change
            table[4, column] -= FORMATION_HEAT[species] * mass_change
    return table


TABLE = make_table()


def lane_weights():
    whole = (672.0, -168.0, 32.0, -3.0)
    inner = np.zeros((LY, LY))
    for out in range(LY):
        for m in range(1, 5):
            if out + m < LY:
                inner[out + m, out] += whole[m - 1]
            if out - m >= 0:
                inner[out - m, out] -= whole[m - 1]
    edge = np.zeros((2 * NF, 2 * LY, LY))
    for field in range(NF):
        for half in range(2):
            base = 8 * field + 4 * half
            for near in range(1, 5):
                for cell in range(1, 6 - near):
                    weight = whole[near + cell - 2]
                    edge[2 * field + half, base + 4 - near, cell - 1] = -weight
                    edge[2 * field + half, LY + base + near - 1, LY - cell] = weight
    return np.concatenate([inner, inner]).astype(jnp.bfloat16), edge.astype(jnp.bfloat16)


def rounded(x):
    return x.astype(BF16).astype(F32)


def shaped(h):
    q1 = rounded(h[0])
    e1 = q1 - h[0]
    q2 = rounded(h[1] + 4.0 * e1)
    left = C[0] * e1 + C[1] * (q2 - h[1])
    q3 = rounded(h[2] - left * (1.0 / C[2]))
    left = left + C[2] * (q3 - h[2])
    return q1, q2, q3, h[3] - left * (1.0 / C[3])


def shaped_lanes(x, layer, turn):
    roll = lambda a, n: pltpu.roll(a, (turn * n) % LY, 1)
    q1 = rounded(x)
    e1 = jnp.where(layer == 0, q1 - x, 0.0)
    q2 = rounded(x + 4.0 * roll(e1, 1))
    e2 = jnp.where(layer == 1, q2 - x, 0.0)
    left = C[0] * roll(e1, 1) + C[1] * e2
    left = roll(left, 1)
    q3 = rounded(x - left * (1.0 / C[2]))
    left = roll(jnp.where(layer == 2, left + C[2] * (q3 - x), 0.0), 1)
    q4 = rounded(x - left * (1.0 / C[3]))
    return jnp.where(layer == 0, q1, jnp.where(layer == 1, q2, jnp.where(layer == 2, q3, q4)))


def kernel(
    f_hbm, r_hbm, wd, wu, fo, ro, mo,
    VEL, PR, PX, TX, YH, NS, NZS, CV, M,
    xps, xpr, dgs, dgr, ys, yr, xs, xr,
    load_sem, xp_ss, xp_rs, dg_ss, dg_rs, y_ss, y_rs, x_ss, x_rs, m_ss, m_rs, own_sem,
):
    gx, gy = lax.axis_index("gx"), lax.axis_index("gy")
    nx, ny = lax.axis_size("gx"), lax.axis_size("gy")
    gxs = (lax.rem(gx + nx - 1, nx), lax.rem(gx + 1, nx))
    gys = (lax.rem(gy + ny - 1, ny), lax.rem(gy + 1, ny))

    barrier = pltpu.get_barrier_semaphore()
    partners = [(gxs[0], gy), (gxs[1], gy)]
    partners += [(gxs[a], gys[b]) for a in range(2) for b in range(2)]
    partners += [(gx, lax.rem(gy + d, ny)) for d in range(1, ny)]
    for partner in partners:
        pl.semaphore_signal(barrier, 1, device_id=partner, device_id_type=MESH)

    parts = [(f_hbm, fo, 0, 5), (f_hbm, fo, 9, 1), (f_hbm, fo, 5, 4), (f_hbm, fo, 10, 4), (r_hbm, ro, 0, 14)]
    loads = [
        pltpu.make_async_copy(a.at[pl.ds(s, n)], b.at[pl.ds(s, n)], load_sem.at[i])
        for i, (a, b, s, n) in enumerate(parts)
    ]
    for load in loads:
        load.start()
    loads[0].wait()
    loads[1].wait()

    def primitive(z, carry):
        rows = pl.ds(pl.multiple_of(z * CX, CX), CX)
        mine = pl.ds(pl.multiple_of(z * 32 + 8, 8), CX)
        inverse = 1.0 / fo[0, rows]
        moment = [fo[1 + d, rows] for d in range(3)]
        speed = [m * inverse for m in moment]
        PR[rows] = 0.4 * (fo[4, rows] - 0.5 * (moment[0] * speed[0] + moment[1] * speed[1] + moment[2] * speed[2]))
        PX[0, mine] = rounded(4.0 * (fo[9, rows] * inverse))
        for d in range(3):
            VEL[d, rows] = speed[d]
            PX[1 + d, mine] = rounded(speed[d])
        return carry

    lax.fori_loop(0, NZ, primitive, 0)

    lane48 = lax.broadcasted_iota(jnp.int32, (NZ, LY), 1)
    eye48 = lane48 == lax.broadcasted_iota(jnp.int32, (NZ, LY), 0)
    for side, (near, far) in enumerate(((0, 1), (15, 14))):
        xps[side, 0] = PX[0, pl.ds(8 + near, NZ, stride=32)].astype(BF16)
        xps[side, 1] = PX[0, pl.ds(8 + far, NZ, stride=32)].astype(BF16)
        for d in range(3):
            xps[side, 2 + d] = PX[1 + d, pl.ds(8 + near, NZ, stride=32)].astype(BF16)
        edge = PX[0, pl.ds(8 + near, NZ, stride=32)]
        for along, lane in enumerate((0, LY - 1)):
            column = jnp.sum(jnp.where(lane48 == lane, edge, 0.0), axis=1, keepdims=True)
            line = jnp.sum(jnp.where(eye48, column, 0.0), axis=0, keepdims=True)
            dgs[2 * side + along] = jnp.broadcast_to(line, (16, LY)).astype(BF16)

    pl.semaphore_wait(barrier, len(partners))

    def remote(src, dst, ss, rs, device):
        return pltpu.make_async_remote_copy(
            src_ref=src, dst_ref=dst, send_sem=ss, recv_sem=rs, device_id=device, device_id_type=MESH
        )

    xp_copy = [remote(xps.at[s], xpr.at[s], xp_ss.at[s], xp_rs.at[s], (gxs[s], gy)) for s in range(2)]
    dg_copy = [
        remote(dgs.at[n], dgr.at[n], dg_ss.at[n], dg_rs.at[n], (gxs[n // 2], gys[n % 2])) for n in range(4)
    ]
    for copy in xp_copy + dg_copy:
        copy.start()
    loads[2].wait()
    loads[3].wait()

    lane = lax.broadcasted_iota(jnp.int32, (CX, LY), 1)
    place = lane & 7
    layer = lane & 3

    def pack_y(i, carry):
        packed = []
        for half in range(2):
            rows = pl.ds(pl.multiple_of(half * HALF + i * CX, CX), CX)
            mine = pl.ds(pl.multiple_of((half * (NZ // 2) + i) * 32 + 8, 8), CX)
            v, p = VEL[1, rows], PR[rows]
            total = jnp.zeros((CX, LY), F32)
            for slot in range(16):
                if slot < NF:
                    flux = fo[slot, rows]
                    flux = (flux + p) * v if slot == 4 else flux * v
                    flux = flux + p if slot == 2 else flux
                elif slot == 14:
                    pu, pv = PX[1, mine], PX[2, mine]
                    flux = jnp.where(lane == 124, pltpu.roll(pu, 125, 1), PX[0, mine])
                    flux = jnp.where(lane == 125, pltpu.roll(pv, 126, 1), flux)
                    flux = jnp.where(lane == 2, pltpu.roll(pu, 2, 1), flux)
                    flux = jnp.where(lane == 3, pltpu.roll(pv, 3, 1), flux)
                else:
                    flux = PX[3, mine]
                total = jnp.where((lane >> 3) == slot, pltpu.roll(flux, (4 + 8 * slot) % LY, 1), total)
            packed.append(total)
        up = jnp.where(place < 4, packed[0], pltpu.roll(packed[1], 4, 1))
        low = jnp.where(place < 4, pltpu.roll(packed[0], LY - 4, 1), packed[1])
        rows = pl.ds(pl.multiple_of(i * CX, CX), CX)
        ys[0, rows] = shaped_lanes(low, layer, 1).astype(BF16)
        ys[1, rows] = shaped_lanes(up, 3 - layer, -1).astype(BF16)
        return carry

    lax.fori_loop(0, NZ // 2, pack_y, 0)
    y_copy = [remote(ys.at[s], yr.at[s], y_ss.at[s], y_rs.at[s], (gx, gys[s])) for s in range(2)]
    for copy in y_copy:
        copy.start()

    def x_copy(side, block):
        return remote(
            xs.at[side, block], xr.at[side, block], x_ss.at[side, block], x_rs.at[side, block], (gxs[side], gy)
        )

    def pack_x(block, carry):
        for side in range(2):
            at = [pl.ds(block * 256 + (n if side == 0 else 15 - n), 16, stride=CX) for n in range(4)]
            u = [VEL[0, a] for a in at]
            for k in range(NF):
                h = []
                for n in range(4):
                    flux = fo[k, at[n]]
                    flux = (flux + PR[at[n]]) * u[n] if k == 4 else flux * u[n]
                    h.append(flux + PR[at[n]] if k == 1 else flux)
                for n, q in enumerate(shaped(h)):
                    xs[side, block, pl.ds((4 * k + n) * 16, 16)] = q.astype(BF16)
            x_copy(side, block).start()
        return carry

    lax.fori_loop(0, 3, pack_x, 0)

    loads[4].wait()

    def chemistry(z, carry):
        rows = pl.ds(pl.multiple_of(z * CX, CX), CX)
        moles = [fo[5 + k, rows] * (18.0 / MOLAR_MASS[k]) for k in range(9)]
        total = moles[0]
        for k in range(1, 9):
            total = total + moles[k]
        cold = (0.25 * total) / PR[rows]
        rates = [
            record[3] * jnp.exp(-record[4] * cold) * (moles[record[0]] * moles[record[1]]) for record in REACTIONS
        ]
        for k in range(NF):
            result = DECAY * ro[k, rows]
            for r in range(8):
                if TABLE[k, r] != 0.0:
                    result = result + float(STEP * TABLE[k, r]) * rates[r]
            ro[k, rows] = result
        return carry

    lax.fori_loop(0, NZ, chemistry, 0)

    for s in range(2):
        xp_copy[s].wait_recv()
    for side, near, far in ((1, 7, 6), (0, 24, 25)):
        PX[0, pl.ds(near, NZ, stride=32)] = xpr[side, 0].astype(F32)
        PX[0, pl.ds(far, NZ, stride=32)] = xpr[side, 1].astype(F32)
        for d in range(3):
            PX[1 + d, pl.ds(near, NZ, stride=32)] = xpr[side, 2 + d].astype(F32)
    for n in range(4):
        dg_copy[n].wait_recv()
    for side, row in ((1, 7), (0, 24)):
        corner = []
        for along in (1, 0):
            line = dgr[2 * side + along].astype(F32)[0:1]
            corner.append(jnp.sum(jnp.where(eye48, line, 0.0), axis=1, keepdims=True))
        TX[pl.ds(row, NZ, stride=32)] = jnp.where(lane48 < 64, corner[0], corner[1])
    for s in range(2):
        y_copy[s].wait_recv()

    def turned(i, carry):
        for half in range(2):
            z = half * (NZ // 2) + i
            rows = pl.ds(pl.multiple_of(z * CX, CX), CX)
            mine = pl.ds(pl.multiple_of(z * 32 + 8, 8), CX)
            there = pl.ds(pl.multiple_of(i * CX, CX), CX)
            low, high = yr[1, there].astype(F32), yr[0, there].astype(F32)
            base = 112 + 4 * half
            put = lambda a, source, target: pltpu.roll(a, (target - source) % LY, 1)
            s = PX[0, mine]
            t = jnp.where(lane < 64, pltpu.roll(s, 2, 1), pltpu.roll(s, LY - 2, 1))
            t = jnp.where(lane < 2, put(low, base + 2, 0), t)
            TX[mine] = jnp.where(lane >= 126, put(high, base, 126), t)
            YH[0, rows] = jnp.where(lane < 64, put(low, base, 0), put(high, base + 2, 127))
            YH[1, rows] = jnp.where(lane < 64, put(low, base + 1, 0), put(high, base + 3, 127))
            YH[2, rows] = jnp.where(lane < 64, put(low, base + 11, 0), put(high, base + 8, 127))
        return carry

    lax.fori_loop(0, NZ // 2, turned, 0)

    def normals(z, carry):
        above, below = lax.rem(z + 1, NZ), lax.rem(z + NZ - 1, NZ)
        rows = pl.ds(pl.multiple_of(z * CX, CX), CX)

        def wide(ref, plane, shift):
            return ref[0, pl.ds(plane * 32 + 4 + shift, 24)]

        def mine(plane, shift=0):
            return pl.ds(plane * 32 + 8 + shift, CX)

        lane24 = lax.broadcasted_iota(jnp.int32, (24, LY), 1)
        s, t = wide(PX, z, 0), TX[pl.ds(z * 32 + 4, 24)]
        behind = jnp.where(lane24 == 0, pltpu.roll(t, LY - 1, 1), pltpu.roll(s, 1, 1))
        ahead = jnp.where(lane24 == LY - 1, pltpu.roll(t, 1, 1), pltpu.roll(s, LY - 1, 1))
        grad_x = 0.5 * (wide(PX, z, 1) - wide(PX, z, -1))
        grad_y = 0.5 * (ahead - behind)
        grad_z = 0.5 * (wide(PX, above, 0) - wide(PX, below, 0))
        scale = -lax.rsqrt(jnp.maximum(grad_x * grad_x + grad_y * grad_y + grad_z * grad_z, 0.01))
        NS[0], NS[1], NS[2] = grad_x * scale, grad_y * scale, grad_z * scale
        normal = [NS[d, 4:20] for d in range(3)]

        t = TX[mine(z)]
        edge_x = 0.5 * (TX[mine(z, 1)] - TX[mine(z, -1)])
        edge_y = 0.5 * (pltpu.roll(t, LY - 1, 1) - pltpu.roll(t, 1, 1))
        edge_z = 0.5 * (TX[mine(above)] - TX[mine(below)])
        edge = -edge_y * lax.rsqrt(jnp.maximum(edge_x * edge_x + edge_y * edge_y + edge_z * edge_z, 0.01))
        behind = jnp.where(lane == 0, pltpu.roll(edge, LY - 1, 1), pltpu.roll(normal[1], 1, 1))
        ahead = jnp.where(lane == LY - 1, pltpu.roll(edge, 1, 1), pltpu.roll(normal[1], LY - 1, 1))
        CV[rows] = 0.5 * (NS[0, 5:21] - NS[0, 3:19]) + 0.5 * (ahead - behind)
        NZS[rows] = normal[2]

        strain = None
        for d in range(3):
            speed, halo = PX[1 + d, mine(z)], YH[d, rows]
            behind = jnp.where(lane == 0, halo, pltpu.roll(speed, 1, 1))
            ahead = jnp.where(lane == LY - 1, halo, pltpu.roll(speed, LY - 1, 1))
            along = (
                0.5 * (PX[1 + d, mine(z, 1)] - PX[1 + d, mine(z, -1)]),
                0.5 * (ahead - behind),
                0.5 * (PX[1 + d, mine(above)] - PX[1 + d, mine(below)]),
            )
            inner = normal[0] * along[0] + normal[1] * along[1] + normal[2] * along[2]
            term = along[d] - normal[d] * inner
            strain = term if strain is None else strain + term
        for d in range(3):
            M[d, z] = normal[d].astype(BF16)
        M[4, z] = strain.astype(BF16)
        return carry

    lax.fori_loop(0, NZ, normals, 0)

    depth = NZ // 8

    def curve(z, carry):
        above, below = lax.rem(z + 1, NZ), lax.rem(z + NZ - 1, NZ)
        at = lambda plane: pl.ds(pl.multiple_of(plane * CX, CX), CX)
        M[3, z] = (CV[at(z)] + 0.5 * (NZS[at(above)] - NZS[at(below)])).astype(BF16)
        return carry

    lax.fori_loop(0, NZ, curve, 0)
    land = mo.at[:, :, :, pl.ds(pl.multiple_of(gy * LY, LY), LY)]

    def m_copy(d):
        target = lax.rem(gy + d, ny)
        return remote(M.at[:, pl.ds(target * depth, depth)], land, m_ss.at[d], m_rs.at[d], (gx, target))

    for d in range(1, 8):
        m_copy(d).start()
    own = pltpu.make_async_copy(M.at[:, pl.ds(gy * depth, depth)], land, own_sem)
    own.start()

    def pass_x(block, carry):
        at = [pl.ds(block * 128 + r, 8, stride=CX) for r in range(CX)]
        u = [VEL[0, a] for a in at]
        for k in range(NF):
            flux = [fo[k, a] for a in at]
            if k == 4:
                flux = [flux[r] + PR[at[r]] for r in range(CX)]
            flux = [flux[r] * u[r] for r in range(CX)]
            if k == 1:
                flux = [flux[r] + PR[at[r]] for r in range(CX)]
            for r in range(CX):
                result = ro[k, at[r]]
                for m in range(1, 5):
                    if r + m < CX and r - m >= 0:
                        result = result - (STEP * C[m - 1]) * (flux[r + m] - flux[r - m])
                    elif r + m < CX:
                        result = result - (STEP * C[m - 1]) * flux[r + m]
                    elif r - m >= 0:
                        result = result + (STEP * C[m - 1]) * flux[r - m]
                ro[k, at[r]] = result
        return carry

    lax.fori_loop(0, NZ // 8, pass_x, 0)

    def pass_z(i, carry):
        first, tile = lax.div(i, 2) * 8, lax.rem(i, 2) * 8
        at = [
            pl.ds(pl.multiple_of(lax.rem(first + (j + NZ - 4), NZ) * CX + tile, 8), 8) for j in range(16)
        ]
        w = [VEL[2, a] for a in at]
        for k in range(NF):
            flux = [fo[k, a] for a in at]
            if k == 4:
                flux = [flux[j] + PR[at[j]] for j in range(16)]
            flux = [flux[j] * w[j] for j in range(16)]
            if k == 3:
                flux = [flux[j] + PR[at[j]] for j in range(16)]
            for j in range(4, 12):
                result = ro[k, at[j]]
                for m in range(1, 5):
                    result = result - (STEP * C[m - 1]) * (flux[j + m] - flux[j - m])
                ro[k, at[j]] = result
        return carry

    lax.fori_loop(0, NZ // 4, pass_z, 0)

    def pass_y(half, carry):
        rows = pl.ds(pl.multiple_of(half * HALF, HALF), HALF)
        edges = jnp.concatenate([yr[1], yr[0]], axis=1)
        for k in range(NF):
            value, v = fo[k, rows], VEL[1, rows]
            flux = (value + PR[rows]) * v if k == 4 else value * v
            flux = flux + PR[rows] if k == 2 else flux
            high = flux.astype(BF16)
            rest = (flux - high.astype(F32)).astype(BF16)
            slope = jnp.dot(jnp.concatenate([high, rest], axis=1), wd[...], preferred_element_type=F32)
            slope = slope + jnp.dot(edges, wu[2 * k + half], preferred_element_type=F32)
            result = ro[k, rows] - (STEP / 840.0) * slope
            ro[k, rows] = result
            fo[k, rows] = value + WEIGHT * result
        return carry

    lax.fori_loop(0, 2, pass_y, 0)

    def pass_edge(block, carry):
        for side in range(2):
            copy = x_copy(side, block)
            copy.wait_recv()
            sign = STEP if side == 1 else -STEP
            for k in range(NF):
                q = [xr[side, block, pl.ds((4 * k + n) * 16, 16)].astype(F32) for n in range(4)]
                for cell in range(4):
                    change = None
                    for n in range(4 - cell):
                        term = (sign * C[n + cell]) * q[n]
                        change = term if change is None else change + term
                    at = pl.ds(block * 256 + (cell if side == 1 else 15 - cell), 16, stride=CX)
                    ro[k, at] = ro[k, at] + change
                    fo[k, at] = fo[k, at] + WEIGHT * change
        return carry

    lax.fori_loop(0, 3, pass_edge, 0)

    for copy in xp_copy + dg_copy + y_copy:
        copy.wait_send()
    for side in range(2):
        for block in range(3):
            x_copy(side, block).wait_send()
    own.wait()
    for d in range(1, 8):
        m_copy(d).wait()


def per_device(fields, register):
    inner, edge = lane_weights()
    flat = lambda a: a.reshape(NF, ROWS, LY)
    any_space, vmem = pl.BlockSpec(memory_space=pl.ANY), pl.BlockSpec(memory_space=pltpu.VMEM)
    dma = pltpu.SemaphoreType.DMA
    big = jax.ShapeDtypeStruct((NF, ROWS, LY), F32)
    fields_next, register_next, metrics = pl.pallas_call(
        kernel,
        out_shape=(
            pltpu.VMEM(big.shape, big.dtype),
            pltpu.VMEM(big.shape, big.dtype),
            jax.ShapeDtypeStruct((5, 6, CX, 1024), BF16),
        ),
        in_specs=[any_space, any_space, vmem, vmem],
        out_specs=(vmem, vmem, any_space),
        scratch_shapes=[
            pltpu.VMEM((3, ROWS, LY), F32),
            pltpu.VMEM((ROWS, LY), F32),
            pltpu.VMEM((4, NZ * 32, LY), F32),
            pltpu.VMEM((NZ * 32, LY), F32),
            pltpu.VMEM((3, ROWS, LY), F32),
            pltpu.VMEM((3, 24, LY), F32),
            pltpu.VMEM((ROWS, LY), F32),
            pltpu.VMEM((ROWS, LY), F32),
            pltpu.VMEM((5, NZ, CX, LY), BF16),
            pltpu.VMEM((2, 5, NZ, LY), BF16),
            pltpu.VMEM((2, 5, NZ, LY), BF16),
            pltpu.VMEM((4, 16, LY), BF16),
            pltpu.VMEM((4, 16, LY), BF16),
            pltpu.VMEM((2, HALF, LY), BF16),
            pltpu.VMEM((2, HALF, LY), BF16),
            pltpu.VMEM((2, 3, NF * 64, LY), BF16),
            pltpu.VMEM((2, 3, NF * 64, LY), BF16),
            dma((5,)),
            dma((2,)),
            dma((2,)),
            dma((4,)),
            dma((4,)),
            dma((2,)),
            dma((2,)),
            dma((2, 3)),
            dma((2, 3)),
            dma((8,)),
            dma((8,)),
            dma(()),
        ],
        compiler_params=pltpu.CompilerParams(collective_id=0, has_side_effects=True, vmem_limit_bytes=44 << 20),
    )(flat(fields), flat(register), jnp.asarray(inner), jnp.asarray(edge))
    shape = fields.shape
    return fields_next.reshape(shape), register_next.reshape(shape), metrics


def solution(mesh):
    in_specs = (P(None, None, "gx", "gy"), P(None, None, "gx", "gy"))
    out_specs = (P(None, None, "gx", "gy"), P(None, None, "gx", "gy"), P(None, "gy", "gx", None))
    return jax.shard_map(per_device, mesh=mesh, in_specs=in_specs, out_specs=out_specs, check_vma=False)
```

time: 276 us -> 74.3 us (0.27)
  the two profiles are of different devices: /device:TPU:1 before, /device:TPU:0 now
where the time goes in v1:
time: 74.3 us; the launch traced here: 74.1 us
  Pallas kernels  67.6 us (91%)
  local copies, waits for them, and re-layouts  5.84 us (8%)
    pallas_call x1, Pallas kernels, per_device(): pl.pallas_call(kernel, out_shape=(pltpu.VMEM(big.shape, big.dtype), pltpu...  67.6 us
    unnamed x5, local copies, waits for them, and re-layouts  5.84 us

profile of v1, /device:TPU:0, one launch (start us, length us, event | category | flops | bytes accessed | tf_op | source)
XLA Modules:
  0.0 74.1 jit_solution(3722729468538548015)
XLA Ops:
  0.6 67.6 %shard_map.67 = (f32[14,768,128]{2,1,0:T(8,128)S(1)}, f32[14,768,128]{2,1,0:T(8,128)S(1)}, bf16[5,6,16,1024]{3,2,1,0:T(8,128)(2,1)}) custom-call(f32[14,768,128]{2,1,0:T(8,128)} %bitcast.6, f32[14,768,128]{2,1,0:T(8,128)} %bitcast.7, bf16[256,128]{1,0:T(8,128)(2,1)} %constant.4.clone.wd, bf16[28,256,128]{2,1,0:T(8,128)(2,1)} %constant.5.clone.wu), custom_call_target="tpu_custom_call" | custom-call | tf_op jit(solution)/shard_map/pallas_call | solution.py:461
  68.3 2.4 %copy.10 = f32[14,48,16,128]{3,2,1,0:T(8,128)} copy(f32[14,48,16,128]{3,2,1,0:T(8,128)S(1)} %bitcast.5) | data formatting | bytes 11010048
  70.7 0.0 copy-start
  70.7 2.4 %copy.11 = f32[14,48,16,128]{3,2,1,0:T(8,128)} copy(f32[14,48,16,128]{3,2,1,0:T(8,128)S(1)} %bitcast.4) | data formatting | bytes 11010048
  73.2 0.0 copy-done
  73.2 0.9 %copy.12 = bf16[5,6,16,1024]{3,2,1,0:T(8,128)(2,1)} copy(bf16[5,6,16,1024]{3,2,1,0:T(8,128)(2,1)S(1)} %copy-done) | data formatting | bytes 1966080
Async XLA Ops:
  70.7 2.4 %copy-start = (bf16[5,6,16,1024]{3,2,1,0:T(8,128)(2,1)S(1)}, bf16[5,6,16,1024]{3,2,1,0:T(8,128)(2,1)}, u32[]{:S(2)}) copy-start(bf16[5,6,16,1024]{3,2,1,0:T(8,128)(2,1)} %get-tuple-element.17) | copy-start | bytes 2949124

commit v2 on v1

v2 whole, which is shorter than its diff:
```python
import jax
import jax.numpy as jnp
import numpy as np
from jax import lax
from jax.experimental import pallas as pl
from jax.experimental.pallas import tpu as pltpu
from jax.sharding import PartitionSpec as P

MESH = pl.DeviceIdType.MESH
F32, BF16 = jnp.float32, jnp.bfloat16
DECAY = -0.4178904745
STEP = 0.25
WEIGHT = 0.3792103129
C = (0.8, -0.2, 4.0 / 105.0, -1.0 / 280.0)
MOLAR_MASS = (2.0, 32.0, 16.0, 17.0, 18.0, 1.0, 33.0, 34.0, 28.0)
FORMATION_HEAT = (0.0, 0.0, 2.0, 0.3, -1.5, 3.0, 0.1, -0.4, 0.0)
REACTIONS = (
    (5, 1, (2, 3), 40.0, 2.0),
    (2, 0, (5, 3), 30.0, 1.2),
    (3, 0, (5, 4), 25.0, 0.8),
    (2, 4, (3, 3), 10.0, 1.6),
    (5, 1, (6,), 15.0, 0.2),
    (6, 5, (3, 3), 20.0, 0.3),
    (6, 6, (7, 1), 12.0, 0.4),
    (7, 8, (3, 3, 8), 8.0, 1.8),
)
NF, NZ, CX, LY = 14, 48, 16, 128
ROWS = NZ * CX
HALF = ROWS // 2


def make_table():
    table = np.zeros((14, 8))
    for column, record in enumerate(REACTIONS):
        change = np.zeros(9)
        change[record[0]] -= 1.0
        change[record[1]] -= 1.0
        for product in record[2]:
            change[product] += 1.0
        for species in range(9):
            mass_change = MOLAR_MASS[species] / 18.0 * change[species]
            table[5 + species, column] = mass_change
            table[4, column] -= FORMATION_HEAT[species] * mass_change
    return table


TABLE = make_table()


WHOLE = (672.0, -168.0, 32.0, -3.0)


def fill_weights(wd, wu):
    gap = lax.broadcasted_iota(jnp.int32, (LY, LY), 0) - lax.broadcasted_iota(jnp.int32, (LY, LY), 1)
    inner = jnp.zeros((LY, LY), F32)
    for m in range(1, 5):
        inner = jnp.where(gap == m, WHOLE[m - 1], jnp.where(gap == -m, -WHOLE[m - 1], inner))
    wd[0:LY] = inner.astype(BF16)
    wd[LY : 2 * LY] = inner.astype(BF16)

    def clear(i, carry):
        wu[i] = jnp.zeros((2 * LY, LY), BF16)
        return carry

    lax.fori_loop(0, 2 * NF, clear, 0)
    row, lane = lax.broadcasted_iota(jnp.int32, (16, LY), 0), lax.broadcasted_iota(jnp.int32, (16, LY), 1)
    tiles = []
    for offset in range(0, 16, 4):
        layer = row - offset
        low, high = jnp.zeros((16, LY), F32), jnp.zeros((16, LY), F32)
        for n in range(4):
            low = jnp.where(layer - lane == n, -WHOLE[3 - n], low)
            high = jnp.where(layer + (LY - 1) - lane == n, WHOLE[n], high)
        valid = (layer >= 0) & (layer < 4)
        tiles.append([jnp.where(valid, t, 0.0).astype(BF16) for t in (low, high)])
    for k in range(NF):
        for half in range(2):
            base = 8 * k + 4 * half
            first = base // 16 * 16
            wu[2 * k + half, first : first + 16] = tiles[base % 16 // 4][0]
            wu[2 * k + half, LY + first : LY + first + 16] = tiles[base % 16 // 4][1]


def rounded(x):
    return x.astype(BF16).astype(F32)


def shaped(h):
    q1 = rounded(h[0])
    e1 = q1 - h[0]
    q2 = rounded(h[1] + 4.0 * e1)
    left = C[0] * e1 + C[1] * (q2 - h[1])
    q3 = rounded(h[2] - left * (1.0 / C[2]))
    left = left + C[2] * (q3 - h[2])
    return q1, q2, q3, h[3] - left * (1.0 / C[3])


def shaped_lanes(x, layer, turn):
    roll = lambda a, n: pltpu.roll(a, (turn * n) % LY, 1)
    q1 = rounded(x)
    e1 = jnp.where(layer == 0, q1 - x, 0.0)
    q2 = rounded(x + 4.0 * roll(e1, 1))
    e2 = jnp.where(layer == 1, q2 - x, 0.0)
    left = C[0] * roll(e1, 1) + C[1] * e2
    left = roll(left, 1)
    q3 = rounded(x - left * (1.0 / C[2]))
    left = roll(jnp.where(layer == 2, left + C[2] * (q3 - x), 0.0), 1)
    q4 = rounded(x - left * (1.0 / C[3]))
    return jnp.where(layer == 0, q1, jnp.where(layer == 1, q2, jnp.where(layer == 2, q3, q4)))


def loop(count, body, unroll):
    def several(i, carry):
        for j in range(unroll):
            body(i * unroll + j, j)
        return carry

    lax.fori_loop(0, count // unroll, several, 0)


def kernel(
    f_hbm, r_hbm, fo, ro, mo,
    wd, wu, VEL, PR, PX, TX, YH, NS, NZS, CV, M,
    xps, xpr, dgs, dgr, yps, ypr, PY, ys, yr, xs, xr,
    load_sem, xp_ss, xp_rs, dg_ss, dg_rs, yp_ss, yp_rs, y_ss, y_rs, x_ss, x_rs, m_ss, m_rs, own_sem,
):
    gx, gy = lax.axis_index("gx"), lax.axis_index("gy")
    nx, ny = lax.axis_size("gx"), lax.axis_size("gy")
    gxs = (lax.rem(gx + nx - 1, nx), lax.rem(gx + 1, nx))
    gys = (lax.rem(gy + ny - 1, ny), lax.rem(gy + 1, ny))

    barrier = pltpu.get_barrier_semaphore()
    partners = [(gxs[0], gy), (gxs[1], gy)]
    partners += [(gxs[a], gys[b]) for a in range(2) for b in range(2)]
    partners += [(gx, lax.rem(gy + d, ny)) for d in range(1, ny)]
    for partner in partners:
        pl.semaphore_signal(barrier, 1, device_id=partner, device_id_type=MESH)

    loads = [
        pltpu.make_async_copy(f_hbm.at[:, pl.ds(n * 256, 256)], fo.at[:, pl.ds(n * 256, 256)], load_sem.at[n])
        for n in range(3)
    ]
    loads.append(pltpu.make_async_copy(r_hbm, ro, load_sem.at[3]))
    for load in loads:
        load.start()

    def remote(src, dst, ss, rs, device):
        return pltpu.make_async_remote_copy(
            src_ref=src, dst_ref=dst, send_sem=ss, recv_sem=rs, device_id=device, device_id_type=MESH
        )

    def primitive(z, _):
        rows = pl.ds(pl.multiple_of(z * CX, CX), CX)
        mine = pl.ds(pl.multiple_of(z * 32 + 8, 8), CX)
        inverse = 1.0 / fo[0, rows]
        moment = [fo[1 + d, rows] for d in range(3)]
        speed = [m * inverse for m in moment]
        PR[rows] = 0.4 * (fo[4, rows] - 0.5 * (moment[0] * speed[0] + moment[1] * speed[1] + moment[2] * speed[2]))
        PX[0, mine] = rounded(4.0 * (fo[9, rows] * inverse))
        for d in range(3):
            VEL[d, rows] = speed[d]
            PX[1 + d, mine] = rounded(speed[d])

    def x_copy(side, block):
        return remote(
            xs.at[side, block], xr.at[side, block], x_ss.at[side, block], x_rs.at[side, block], (gxs[side], gy)
        )

    def pack_x(block):
        for side in range(2):
            at = [pl.ds(block * 256 + (n if side == 0 else 15 - n), 16, stride=CX) for n in range(4)]
            u = [VEL[0, a] for a in at]
            for k in range(NF):
                h = []
                for n in range(4):
                    flux = fo[k, at[n]]
                    flux = (flux + PR[at[n]]) * u[n] if k == 4 else flux * u[n]
                    h.append(flux + PR[at[n]] if k == 1 else flux)
                for n, q in enumerate(shaped(h)):
                    xs[side, block, pl.ds((4 * k + n) * 16, 16)] = q.astype(BF16)

    def send_x(block):
        for side in range(2):
            x_copy(side, block).start()

    loads[0].wait()
    loop(16, primitive, 4)
    pack_x(0)
    pl.semaphore_wait(barrier, len(partners))
    send_x(0)
    loads[1].wait()
    loads[2].wait()
    loop(32, lambda z, _: primitive(z + 16, _), 4)

    lane48 = lax.broadcasted_iota(jnp.int32, (NZ, LY), 1)
    eye48 = lane48 == lax.broadcasted_iota(jnp.int32, (NZ, LY), 0)
    for side, (near, far) in enumerate(((0, 1), (15, 14))):
        xps[side, 0] = PX[0, pl.ds(8 + near, NZ, stride=32)].astype(BF16)
        xps[side, 1] = PX[0, pl.ds(8 + far, NZ, stride=32)].astype(BF16)
        for d in range(3):
            xps[side, 2 + d] = PX[1 + d, pl.ds(8 + near, NZ, stride=32)].astype(BF16)
        edge = PX[0, pl.ds(8 + near, NZ, stride=32)]
        for along, lane in enumerate((0, LY - 1)):
            column = jnp.sum(jnp.where(lane48 == lane, edge, 0.0), axis=1, keepdims=True)
            line = jnp.sum(jnp.where(eye48, column, 0.0), axis=0, keepdims=True)
            dgs[2 * side + along] = jnp.broadcast_to(line, (16, LY)).astype(BF16)

    xp_copy = [remote(xps.at[s], xpr.at[s], xp_ss.at[s], xp_rs.at[s], (gxs[s], gy)) for s in range(2)]
    dg_copy = [
        remote(dgs.at[n], dgr.at[n], dg_ss.at[n], dg_rs.at[n], (gxs[n // 2], gys[n % 2])) for n in range(4)
    ]
    for copy in xp_copy + dg_copy:
        copy.start()

    lane = lax.broadcasted_iota(jnp.int32, (CX, LY), 1)

    def pack_probe(block, _):
        packed = []
        for half in range(2):
            total = None
            for j in range(8):
                mine = pl.ds(pl.multiple_of((half * (NZ // 2) + block * 8 + j) * 32 + 8, 8), CX)
                face = PX[0, mine]
                for d in range(3):
                    speed = PX[1 + d, mine]
                    face = jnp.where(lane == 2 + d, pltpu.roll(speed, 2 + d, 1), face)
                    face = jnp.where(lane == 125 - d, pltpu.roll(speed, LY - 2 - d, 1), face)
                face = pltpu.roll(face, (16 * j + 8) % LY, 1)
                total = face if total is None else jnp.where((lane >> 4) == j, face, total)
            packed.append(total)
        rows = pl.ds(pl.multiple_of(block * CX, CX), CX)
        first = (lane & 15) < 8
        yps[0, rows] = jnp.where(first, pltpu.roll(packed[0], LY - 8, 1), packed[1]).astype(BF16)
        yps[1, rows] = jnp.where(first, packed[0], pltpu.roll(packed[1], 8, 1)).astype(BF16)

    loop(3, pack_probe, 1)
    yp_copy = [remote(yps.at[s], ypr.at[s], yp_ss.at[s], yp_rs.at[s], (gx, gys[s])) for s in range(2)]
    for copy in yp_copy:
        copy.start()
    def later_x(block, carry):
        pack_x(block)
        send_x(block)
        return carry

    lax.fori_loop(1, 3, later_x, 0)

    place = lane & 7
    layer = lane & 3

    def pack_y(i, _):
        packed = []
        for half in range(2):
            rows = pl.ds(pl.multiple_of(half * HALF + i * CX, CX), CX)
            v, p = VEL[1, rows], PR[rows]
            total = jnp.zeros((CX, LY), F32)
            for slot in range(NF):
                flux = fo[slot, rows]
                flux = (flux + p) * v if slot == 4 else flux * v
                flux = flux + p if slot == 2 else flux
                total = jnp.where((lane >> 3) == slot, pltpu.roll(flux, (4 + 8 * slot) % LY, 1), total)
            packed.append(total)
        rows = pl.ds(pl.multiple_of(i * CX, CX), CX)
        PY[0, rows] = jnp.where(place < 4, pltpu.roll(packed[0], LY - 4, 1), packed[1])
        PY[1, rows] = jnp.where(place < 4, packed[0], pltpu.roll(packed[1], 4, 1))

    loop(NZ // 2, pack_y, 3)
    deep = lax.broadcasted_iota(jnp.int32, (HALF // 4, LY), 1) & 3

    def shape_y(i, _):
        rows = pl.ds(pl.multiple_of(i * (HALF // 4), CX), HALF // 4)
        ys[0, rows] = shaped_lanes(PY[0, rows], deep, 1).astype(BF16)
        ys[1, rows] = shaped_lanes(PY[1, rows], 3 - deep, -1).astype(BF16)

    loop(4, shape_y, 1)
    y_copy = [remote(ys.at[s], yr.at[s], y_ss.at[s], y_rs.at[s], (gx, gys[s])) for s in range(2)]
    for copy in y_copy:
        copy.start()

    fill_weights(wd, wu)

    loads[3].wait()

    def chemistry(z, _):
        rows = pl.ds(pl.multiple_of(z * CX, CX), CX)
        moles = [fo[5 + k, rows] * (18.0 / MOLAR_MASS[k]) for k in range(9)]
        total = moles[0]
        for k in range(1, 9):
            total = total + moles[k]
        cold = (0.25 * total) / PR[rows]
        rates = [
            record[3] * jnp.exp(-record[4] * cold) * (moles[record[0]] * moles[record[1]]) for record in REACTIONS
        ]
        for k in range(NF):
            result = DECAY * ro[k, rows]
            for r in range(8):
                if TABLE[k, r] != 0.0:
                    result = result + float(STEP * TABLE[k, r]) * rates[r]
            ro[k, rows] = result

    loop(NZ, chemistry, 4)

    for s in range(2):
        xp_copy[s].wait_recv()
    for side, near, far in ((1, 7, 6), (0, 24, 25)):
        PX[0, pl.ds(near, NZ, stride=32)] = xpr[side, 0].astype(F32)
        PX[0, pl.ds(far, NZ, stride=32)] = xpr[side, 1].astype(F32)
        for d in range(3):
            PX[1 + d, pl.ds(near, NZ, stride=32)] = xpr[side, 2 + d].astype(F32)
    for n in range(4):
        dg_copy[n].wait_recv()
    for side, row in ((1, 7), (0, 24)):
        corner = []
        for along in (1, 0):
            line = dgr[2 * side + along].astype(F32)[0:1]
            corner.append(jnp.sum(jnp.where(eye48, line, 0.0), axis=1, keepdims=True))
        TX[pl.ds(row, NZ, stride=32)] = jnp.where(lane48 < 64, corner[0], corner[1])
    for s in range(2):
        yp_copy[s].wait_recv()

    def turned(block, _):
        there = pl.ds(pl.multiple_of(block * CX, CX), CX)
        low, high = ypr[1, there].astype(F32), ypr[0, there].astype(F32)
        put = lambda a, source, target: pltpu.roll(a, (target - source) % LY, 1)
        for half, j in [(half, j) for half in range(2) for j in range(8)]:
            z = half * (NZ // 2) + block * 8 + j
            rows = pl.ds(pl.multiple_of(z * CX, CX), CX)
            mine = pl.ds(pl.multiple_of(z * 32 + 8, 8), CX)
            base = 16 * j + 8 * half
            s = PX[0, mine]
            t = jnp.where(lane < 64, pltpu.roll(s, 2, 1), pltpu.roll(s, LY - 2, 1))
            t = jnp.where(lane < 2, put(low, base + 6, 0), t)
            TX[mine] = jnp.where(lane >= 126, put(high, base, 126), t)
            for d in range(3):
                YH[d, rows] = jnp.where(lane < 64, put(low, base + 5 - d, 0), put(high, base + 2 + d, 127))

    loop(3, turned, 1)

    def normals(z, turn):
        above, below = lax.rem(z + 1, NZ), lax.rem(z + NZ - 1, NZ)
        rows = pl.ds(pl.multiple_of(z * CX, CX), CX)

        def wide(ref, plane, shift):
            return ref[0, pl.ds(plane * 32 + 4 + shift, 24)]

        def mine(plane, shift=0):
            return pl.ds(plane * 32 + 8 + shift, CX)

        lane24 = lax.broadcasted_iota(jnp.int32, (24, LY), 1)
        s, t = wide(PX, z, 0), TX[pl.ds(z * 32 + 4, 24)]
        behind = jnp.where(lane24 == 0, pltpu.roll(t, LY - 1, 1), pltpu.roll(s, 1, 1))
        ahead = jnp.where(lane24 == LY - 1, pltpu.roll(t, 1, 1), pltpu.roll(s, LY - 1, 1))
        grad_x = 0.5 * (wide(PX, z, 1) - wide(PX, z, -1))
        grad_y = 0.5 * (ahead - behind)
        grad_z = 0.5 * (wide(PX, above, 0) - wide(PX, below, 0))
        scale = -lax.rsqrt(jnp.maximum(grad_x * grad_x + grad_y * grad_y + grad_z * grad_z, 0.01))
        NS[turn, 0], NS[turn, 1], NS[turn, 2] = grad_x * scale, grad_y * scale, grad_z * scale
        normal = [NS[turn, d, 4:20] for d in range(3)]

        t = TX[mine(z)]
        edge_x = 0.5 * (TX[mine(z, 1)] - TX[mine(z, -1)])
        edge_y = 0.5 * (pltpu.roll(t, LY - 1, 1) - pltpu.roll(t, 1, 1))
        edge_z = 0.5 * (TX[mine(above)] - TX[mine(below)])
        edge = -edge_y * lax.rsqrt(jnp.maximum(edge_x * edge_x + edge_y * edge_y + edge_z * edge_z, 0.01))
        behind = jnp.where(lane == 0, pltpu.roll(edge, LY - 1, 1), pltpu.roll(normal[1], 1, 1))
        ahead = jnp.where(lane == LY - 1, pltpu.roll(edge, 1, 1), pltpu.roll(normal[1], LY - 1, 1))
        CV[rows] = 0.5 * (NS[turn, 0, 5:21] - NS[turn, 0, 3:19]) + 0.5 * (ahead - behind)
        NZS[rows] = normal[2]

        strain = None
        for d in range(3):
            speed, halo = PX[1 + d, mine(z)], YH[d, rows]
            behind = jnp.where(lane == 0, halo, pltpu.roll(speed, 1, 1))
            ahead = jnp.where(lane == LY - 1, halo, pltpu.roll(speed, LY - 1, 1))
            along = (
                0.5 * (PX[1 + d, mine(z, 1)] - PX[1 + d, mine(z, -1)]),
                0.5 * (ahead - behind),
                0.5 * (PX[1 + d, mine(above)] - PX[1 + d, mine(below)]),
            )
            inner = normal[0] * along[0] + normal[1] * along[1] + normal[2] * along[2]
            term = along[d] - normal[d] * inner
            strain = term if strain is None else strain + term
        for d in range(3):
            M[d, z] = normal[d].astype(BF16)
        M[4, z] = strain.astype(BF16)

    loop(NZ, normals, 3)

    depth = NZ // 8

    def curve(z, _):
        above, below = lax.rem(z + 1, NZ), lax.rem(z + NZ - 1, NZ)
        at = lambda plane: pl.ds(pl.multiple_of(plane * CX, CX), CX)
        M[3, z] = (CV[at(z)] + 0.5 * (NZS[at(above)] - NZS[at(below)])).astype(BF16)

    loop(NZ, curve, 6)
    land = mo.at[:, :, :, pl.ds(pl.multiple_of(gy * LY, LY), LY)]

    def m_copy(d):
        target = lax.rem(gy + d, ny)
        return remote(M.at[:, pl.ds(target * depth, depth)], land, m_ss.at[d], m_rs.at[d], (gx, target))

    for d in range(1, 8):
        m_copy(d).start()
    own = pltpu.make_async_copy(M.at[:, pl.ds(gy * depth, depth)], land, own_sem)
    own.start()

    def pass_z(i, carry):
        first, tile = lax.div(i, 2) * 8, lax.rem(i, 2) * 8
        at = [
            pl.ds(pl.multiple_of(lax.rem(first + (j + NZ - 4), NZ) * CX + tile, 8), 8) for j in range(16)
        ]
        w = [VEL[2, a] for a in at]
        for k in range(NF):
            flux = [fo[k, a] for a in at]
            if k == 4:
                flux = [flux[j] + PR[at[j]] for j in range(16)]
            flux = [flux[j] * w[j] for j in range(16)]
            if k == 3:
                flux = [flux[j] + PR[at[j]] for j in range(16)]
            before = [ro[k, a] for a in at[4:12]]
            after = []
            for j in range(4, 12):
                change = (STEP * C[0]) * (flux[j - 1] - flux[j + 1])
                for m in range(2, 5):
                    change = change + (STEP * C[m - 1]) * (flux[j - m] - flux[j + m])
                after.append(before[j - 4] + change)
            for j in range(4, 12):
                ro[k, at[j]] = after[j - 4]
        return carry

    lax.fori_loop(0, NZ // 4, pass_z, 0)

    def pass_x(block, carry):
        for side in range(2):
            x_copy(side, block).wait_recv()
        for part in range(2):
            at = [pl.ds(block * 256 + part * 128 + r, 8, stride=CX) for r in range(CX)]
            u = [VEL[0, a] for a in at]
            for k in range(NF):
                flux = [fo[k, a] for a in at]
                if k == 4:
                    flux = [flux[r] + PR[at[r]] for r in range(CX)]
                flux = [flux[r] * u[r] for r in range(CX)]
                if k == 1:
                    flux = [flux[r] + PR[at[r]] for r in range(CX)]
                low, high = [
                    [
                        xr[side, block, pl.ds((4 * k + n) * 16, 16)].astype(F32)[8 * part : 8 * part + 8]
                        for n in range(4)
                    ]
                    for side in (1, 0)
                ]
                flux = low[::-1] + flux + high
                before = [ro[k, a] for a in at]
                after = []
                for r in range(CX):
                    change = (STEP * C[0]) * (flux[r + 3] - flux[r + 5])
                    for m in range(2, 5):
                        change = change + (STEP * C[m - 1]) * (flux[r + 4 - m] - flux[r + 4 + m])
                    after.append(before[r] + change)
                for r in range(CX):
                    ro[k, at[r]] = after[r]
        return carry

    lax.fori_loop(0, 3, pass_x, 0)

    for s in range(2):
        y_copy[s].wait_recv()

    def pass_y(half, carry):
        rows = pl.ds(pl.multiple_of(half * HALF, HALF), HALF)
        edges = jnp.concatenate([yr[1], yr[0]], axis=1)
        for k in range(NF):
            value, v = fo[k, rows], VEL[1, rows]
            flux = (value + PR[rows]) * v if k == 4 else value * v
            flux = flux + PR[rows] if k == 2 else flux
            high = flux.astype(BF16)
            rest = (flux - high.astype(F32)).astype(BF16)
            slope = jnp.dot(jnp.concatenate([high, rest], axis=1), wd[...], preferred_element_type=F32)
            slope = slope + jnp.dot(edges, wu[2 * k + half], preferred_element_type=F32)
            result = ro[k, rows] - (STEP / 840.0) * slope
            ro[k, rows] = result
        return carry

    lax.fori_loop(0, 2, pass_y, 0)

    for copy in xp_copy + dg_copy + yp_copy + y_copy:
        copy.wait_send()
    for side in range(2):
        for block in range(3):
            x_copy(side, block).wait_send()
    own.wait()
    for d in range(1, 8):
        m_copy(d).wait()


def place_out(f_in, r_in, m_in, f_out, r_out, m_out, new, sem):
    copies = [
        pltpu.make_async_copy(m_in, m_out, sem.at[0]),
        pltpu.make_async_copy(r_in.at[pl.ds(0, 7)], r_out.at[pl.ds(0, 7)], sem.at[1]),
        pltpu.make_async_copy(r_in.at[pl.ds(7, 7)], r_out.at[pl.ds(7, 7)], sem.at[2]),
    ]
    for copy in copies:
        copy.start()
    for part in range(7):
        for k in (2 * part, 2 * part + 1):

            def update(i, _, k=k):
                rows = pl.ds(pl.multiple_of(i * 192, 192), 192)
                new[k, rows] = f_in[k, rows] + WEIGHT * r_in[k, rows]

            loop(4, update, 1)
        at = pl.ds(2 * part, 2)
        copies.append(pltpu.make_async_copy(new.at[at], f_out.at[at], sem.at[3 + part]))
        copies[-1].start()
    for copy in copies:
        copy.wait()


def per_device(fields, register):
    flat = lambda a: a.reshape(NF, ROWS, LY)
    any_space, vmem = pl.BlockSpec(memory_space=pl.ANY), pl.BlockSpec(memory_space=pltpu.VMEM)
    hbm = pl.BlockSpec(memory_space=pltpu.HBM)
    dma = pltpu.SemaphoreType.DMA
    big = jax.ShapeDtypeStruct((NF, ROWS, LY), F32)
    fields_next, register_next, metrics = pl.pallas_call(
        kernel,
        out_shape=(
            pltpu.VMEM(big.shape, big.dtype),
            pltpu.VMEM(big.shape, big.dtype),
            pltpu.VMEM((5, 6, CX, 1024), BF16),
        ),
        in_specs=[hbm] * 2,
        out_specs=(vmem, vmem, vmem),
        scratch_shapes=[
            pltpu.VMEM((2 * LY, LY), BF16),
            pltpu.VMEM((2 * NF, 2 * LY, LY), BF16),
            pltpu.VMEM((3, ROWS, LY), F32),
            pltpu.VMEM((ROWS, LY), F32),
            pltpu.VMEM((4, NZ * 32, LY), F32),
            pltpu.VMEM((NZ * 32, LY), F32),
            pltpu.VMEM((3, ROWS, LY), F32),
            pltpu.VMEM((3, 3, 24, LY), F32),
            pltpu.VMEM((ROWS, LY), F32),
            pltpu.VMEM((ROWS, LY), F32),
            pltpu.VMEM((5, NZ, CX, LY), BF16),
            pltpu.VMEM((2, 5, NZ, LY), BF16),
            pltpu.VMEM((2, 5, NZ, LY), BF16),
            pltpu.VMEM((4, 16, LY), BF16),
            pltpu.VMEM((4, 16, LY), BF16),
            pltpu.VMEM((2, 48, LY), BF16),
            pltpu.VMEM((2, 48, LY), BF16),
            pltpu.VMEM((2, HALF, LY), F32),
            pltpu.VMEM((2, HALF, LY), BF16),
            pltpu.VMEM((2, HALF, LY), BF16),
            pltpu.VMEM((2, 3, NF * 64, LY), BF16),
            pltpu.VMEM((2, 3, NF * 64, LY), BF16),
            dma((4,)),
            dma((2,)),
            dma((2,)),
            dma((4,)),
            dma((4,)),
            dma((2,)),
            dma((2,)),
            dma((2,)),
            dma((2,)),
            dma((2, 3)),
            dma((2, 3)),
            dma((8,)),
            dma((8,)),
            dma(()),
        ],
        compiler_params=pltpu.CompilerParams(collective_id=0, has_side_effects=True, vmem_limit_bytes=40 << 20),
    )(flat(fields), flat(register))
    small = jax.ShapeDtypeStruct(metrics.shape, BF16)
    fields_next, register_next, metrics = pl.pallas_call(
        place_out,
        out_shape=(big, big, small),
        in_specs=[vmem] * 3,
        out_specs=(any_space,) * 3,
        scratch_shapes=[pltpu.VMEM(big.shape, F32), dma((10,))],
        compiler_params=pltpu.CompilerParams(vmem_limit_bytes=8 << 20),
    )(*(pltpu.with_memory_space_constraint(a, pltpu.VMEM) for a in (fields_next, register_next, metrics)))
    shape = fields.shape
    return fields_next.reshape(shape), register_next.reshape(shape), metrics


def solution(mesh):
    in_specs = (P(None, None, "gx", "gy"), P(None, None, "gx", "gy"))
    out_specs = (P(None, None, "gx", "gy"), P(None, None, "gx", "gy"), P(None, "gy", "gx", None))
    return jax.shard_map(per_device, mesh=mesh, in_specs=in_specs, out_specs=out_specs, check_vma=False)
```

time: 74.3 us -> 47.6 us (0.64)
  the two profiles are of different devices: /device:TPU:0 before, /device:TPU:1 now
where the time goes in v2:
time: 47.6 us; the launch traced here: 47.5 us
  Pallas kernels  46.9 us (99%)
  between operations  0.64 us (1%)
    pallas_call x1, Pallas kernels, per_device(): pl.pallas_call(kernel, out_shape=(pltpu.VMEM(big.shape, big.dtype), pltpu...  42.3 us
    pallas_call x1, Pallas kernels, per_device(): pl.pallas_call(place_out, out_shape=(big, big, small), in_specs=[vmem] *...  4.52 us

profile of v2, /device:TPU:1, one launch (start us, length us, event | category | flops | bytes accessed | tf_op | source)
XLA Modules:
  0.0 47.5 jit_solution(11375106942835970253)
XLA Ops:
  0.6 42.3 %shard_map.49 = (f32[14,768,128]{2,1,0:T(8,128)S(1)}, f32[14,768,128]{2,1,0:T(8,128)S(1)}, bf16[5,6,16,1024]{3,2,1,0:T(8,128)(2,1)S(1)}) custom-call(f32[14,768,128]{2,1,0:T(8,128)} %bitcast.4, f32[14,768,128]{2,1,0:T(8,128)} %bitcast.5), custom_call_target="tpu_custom_call" | custom-call | tf_op jit(solution)/shard_map/pallas_call | solution.py:526
  43.0 4.5 %shard_map.50 = (f32[14,768,128]{2,1,0:T(8,128)}, f32[14,768,128]{2,1,0:T(8,128)}, bf16[5,6,16,1024]{3,2,1,0:T(8,128)(2,1)}) custom-call(f32[14,768,128]{2,1,0:T(8,128)S(1)} %get-tuple-element.9.f_in, f32[14,768,128]{2,1,0:T(8,128)S(1)} %get-tuple-element.10.r_in, bf16[5,6,16,1024]{3,2,1,0:T(8,128)(2,1)S(1)} %get-tuple-element.11.m_in), custom_call_target="tpu_custom_call" | custom-call | tf_op jit(solution)/shard_map/pallas_call | solution.py:576

commit v3 on v2

--- a/solution.py
+++ b/solution.py
@@ -85,10 +85,18 @@
     return x.astype(BF16).astype(F32)
 
 
-def shaped(h):
-    q1 = rounded(h[0])
+KNOWN = {(2, 0): 3, (3, 0): 4, (9, 0): 0, (9, 1): 1}
+SENT = [(k, n) for k in range(NF) for n in range(4) if (k, n) not in KNOWN]
+
+
+def known_flux(k, mass, probe):
+    return mass * probe * 0.25 if k == 9 else mass * probe
+
+
+def shaped(h, given=()):
+    q1 = given[0] if len(given) > 0 else rounded(h[0])
     e1 = q1 - h[0]
-    q2 = rounded(h[1] + 4.0 * e1)
+    q2 = given[1] if len(given) > 1 else rounded(h[1] + 4.0 * e1)
     left = C[0] * e1 + C[1] * (q2 - h[1])
     q3 = rounded(h[2] - left * (1.0 / C[2]))
     left = left + C[2] * (q3 - h[2])
@@ -176,8 +184,17 @@
                     flux = fo[k, at[n]]
                     flux = (flux + PR[at[n]]) * u[n] if k == 4 else flux * u[n]
                     h.append(flux + PR[at[n]] if k == 1 else flux)
-                for n, q in enumerate(shaped(h)):
-                    xs[side, block, pl.ds((4 * k + n) * 16, 16)] = q.astype(BF16)
+                given = []
+                for n in range(2):
+                    if (k, n) in KNOWN:
+                        row = n if side == 0 else 15 - n
+                        probe = PX[{2: 2, 3: 3, 9: 0}[k], pl.ds(block * 512 + 8 + row, 16, stride=32)]
+                        given.append(known_flux(k, mass[n], probe))
+                q = shaped(h, given)
+                mass = q[:2] if k == 0 else mass
+                for n in range(4):
+                    if (k, n) not in KNOWN:
+                        xs[side, block, pl.ds(SENT.index((k, n)) * 16, 16)] = q[n].astype(BF16)
 
     def send_x(block):
         for side in range(2):
@@ -185,9 +202,7 @@
 
     loads[0].wait()
     loop(16, primitive, 4)
-    pack_x(0)
     pl.semaphore_wait(barrier, len(partners))
-    send_x(0)
     loads[1].wait()
     loads[2].wait()
     loop(32, lambda z, _: primitive(z + 16, _), 4)
@@ -242,7 +257,7 @@
         send_x(block)
         return carry
 
-    lax.fori_loop(1, 3, later_x, 0)
+    lax.fori_loop(0, 3, later_x, 0)
 
     place = lane & 7
     layer = lane & 3
@@ -430,6 +445,13 @@
 
     lax.fori_loop(0, NZ // 4, pass_z, 0)
 
+    def layer_x(side, block, k, n, part):
+        half = slice(8 * part, 8 * part + 8)
+        if (k, n) in KNOWN:
+            probe = xpr[side, KNOWN[k, n], pl.ds(pl.multiple_of(block * 16, 16), 16)].astype(F32)[half]
+            return known_flux(k, layer_x(side, block, 0, n, part), probe)
+        return xr[side, block, pl.ds(SENT.index((k, n)) * 16, 16)].astype(F32)[half]
+
     def pass_x(block, carry):
         for side in range(2):
             x_copy(side, block).wait_recv()
@@ -443,13 +465,7 @@
                 flux = [flux[r] * u[r] for r in range(CX)]
                 if k == 1:
                     flux = [flux[r] + PR[at[r]] for r in range(CX)]
-                low, high = [
-                    [
-                        xr[side, block, pl.ds((4 * k + n) * 16, 16)].astype(F32)[8 * part : 8 * part + 8]
-                        for n in range(4)
-                    ]
-                    for side in (1, 0)
-                ]
+                low, high = [[layer_x(side, block, k, n, part) for n in range(4)] for side in (1, 0)]
                 flux = low[::-1] + flux + high
                 before = [ro[k, a] for a in at]
                 after = []
@@ -553,8 +569,8 @@
             pltpu.VMEM((2, HALF, LY), F32),
             pltpu.VMEM((2, HALF, LY), BF16),
             pltpu.VMEM((2, HALF, LY), BF16),
-            pltpu.VMEM((2, 3, NF * 64, LY), BF16),
-            pltpu.VMEM((2, 3, NF * 64, LY), BF16),
+            pltpu.VMEM((2, 3, len(SENT) * 16, LY), BF16),
+            pltpu.VMEM((2, 3, len(SENT) * 16, LY), BF16),
             dma((4,)),
             dma((2,)),
             dma((2,)),

time: 47.6 us -> 45.1 us (0.947)
  Pallas kernels: 46.9 us -> 44.3 us
    pallas_call x1, Pallas kernels: 42.3 us -> 39.8 us  [per_device(): pl.pallas_call(kernel, out_shape=(pltpu.VMEM(big.shape, big.dtype), pltpu...]
where the time goes in v3:
time: 45.1 us; the launch traced here: 45 us
  Pallas kernels  44.3 us (98%)
  between operations  0.64 us (1%)
    pallas_call x1, Pallas kernels, per_device(): pl.pallas_call(kernel, out_shape=(pltpu.VMEM(big.shape, big.dtype), pltpu...  39.8 us
    pallas_call x1, Pallas kernels, per_device(): pl.pallas_call(place_out, out_shape=(big, big, small), in_specs=[vmem] *...  4.52 us

profile of v3, /device:TPU:1, one launch (start us, length us, event | category | flops | bytes accessed | tf_op | source)
XLA Modules:
  0.0 45.0 jit_solution(3441058881052635762)
XLA Ops:
  0.6 39.8 %shard_map.49 = (f32[14,768,128]{2,1,0:T(8,128)S(1)}, f32[14,768,128]{2,1,0:T(8,128)S(1)}, bf16[5,6,16,1024]{3,2,1,0:T(8,128)(2,1)S(1)}) custom-call(f32[14,768,128]{2,1,0:T(8,128)} %bitcast.4, f32[14,768,128]{2,1,0:T(8,128)} %bitcast.5), custom_call_target="tpu_custom_call" | custom-call | tf_op jit(solution)/shard_map/pallas_call | solution.py:542
  40.5 4.5 %shard_map.50 = (f32[14,768,128]{2,1,0:T(8,128)}, f32[14,768,128]{2,1,0:T(8,128)}, bf16[5,6,16,1024]{3,2,1,0:T(8,128)(2,1)}) custom-call(f32[14,768,128]{2,1,0:T(8,128)S(1)} %get-tuple-element.9.f_in, f32[14,768,128]{2,1,0:T(8,128)S(1)} %get-tuple-element.10.r_in, bf16[5,6,16,1024]{3,2,1,0:T(8,128)(2,1)S(1)} %get-tuple-element.11.m_in), custom_call_target="tpu_custom_call" | custom-call | tf_op jit(solution)/shard_map/pallas_call | solution.py:592

commit v4 on v3

--- a/solution.py
+++ b/solution.py
@@ -259,38 +259,6 @@
 
     lax.fori_loop(0, 3, later_x, 0)
 
-    place = lane & 7
-    layer = lane & 3
-
-    def pack_y(i, _):
-        packed = []
-        for half in range(2):
-            rows = pl.ds(pl.multiple_of(half * HALF + i * CX, CX), CX)
-            v, p = VEL[1, rows], PR[rows]
-            total = jnp.zeros((CX, LY), F32)
-            for slot in range(NF):
-                flux = fo[slot, rows]
-                flux = (flux + p) * v if slot == 4 else flux * v
-                flux = flux + p if slot == 2 else flux
-                total = jnp.where((lane >> 3) == slot, pltpu.roll(flux, (4 + 8 * slot) % LY, 1), total)
-            packed.append(total)
-        rows = pl.ds(pl.multiple_of(i * CX, CX), CX)
-        PY[0, rows] = jnp.where(place < 4, pltpu.roll(packed[0], LY - 4, 1), packed[1])
-        PY[1, rows] = jnp.where(place < 4, packed[0], pltpu.roll(packed[1], 4, 1))
-
-    loop(NZ // 2, pack_y, 3)
-    deep = lax.broadcasted_iota(jnp.int32, (HALF // 4, LY), 1) & 3
-
-    def shape_y(i, _):
-        rows = pl.ds(pl.multiple_of(i * (HALF // 4), CX), HALF // 4)
-        ys[0, rows] = shaped_lanes(PY[0, rows], deep, 1).astype(BF16)
-        ys[1, rows] = shaped_lanes(PY[1, rows], 3 - deep, -1).astype(BF16)
-
-    loop(4, shape_y, 1)
-    y_copy = [remote(ys.at[s], yr.at[s], y_ss.at[s], y_rs.at[s], (gx, gys[s])) for s in range(2)]
-    for copy in y_copy:
-        copy.start()
-
     fill_weights(wd, wu)
 
     loads[3].wait()
@@ -313,6 +281,38 @@
             ro[k, rows] = result
 
     loop(NZ, chemistry, 4)
+
+    place = lane & 7
+    layer = lane & 3
+
+    def pack_y(i, _):
+        packed = []
+        for half in range(2):
+            rows = pl.ds(pl.multiple_of(half * HALF + i * CX, CX), CX)
+            v, p = VEL[1, rows], PR[rows]
+            total = jnp.zeros((CX, LY), F32)
+            for slot in range(NF):
+                flux = fo[slot, rows]
+                flux = (flux + p) * v if slot == 4 else flux * v
+                flux = flux + p if slot == 2 else flux
+                total = jnp.where((lane >> 3) == slot, pltpu.roll(flux, (4 + 8 * slot) % LY, 1), total)
+            packed.append(total)
+        rows = pl.ds(pl.multiple_of(i * CX, CX), CX)
+        PY[0, rows] = jnp.where(place < 4, pltpu.roll(packed[0], LY - 4, 1), packed[1])
+        PY[1, rows] = jnp.where(place < 4, packed[0], pltpu.roll(packed[1], 4, 1))
+
+    loop(NZ // 2, pack_y, 3)
+    deep = lax.broadcasted_iota(jnp.int32, (HALF // 4, LY), 1) & 3
+
+    def shape_y(i, _):
+        rows = pl.ds(pl.multiple_of(i * (HALF // 4), CX), HALF // 4)
+        ys[0, rows] = shaped_lanes(PY[0, rows], deep, 1).astype(BF16)
+        ys[1, rows] = shaped_lanes(PY[1, rows], 3 - deep, -1).astype(BF16)
+
+    loop(4, shape_y, 1)
+    y_copy = [remote(ys.at[s], yr.at[s], y_ss.at[s], y_rs.at[s], (gx, gys[s])) for s in range(2)]
+    for copy in y_copy:
+        copy.start()
 
     for s in range(2):
         xp_copy[s].wait_recv()

time: 45.1 us -> 45.1 us (level)
  no operation moved by 1% of the time
where the time goes in v4:
time: 45.1 us; the launch traced here: 45 us
  Pallas kernels  44.3 us (98%)
  between operations  0.64 us (1%)
    pallas_call x1, Pallas kernels, per_device(): pl.pallas_call(kernel, out_shape=(pltpu.VMEM(big.shape, big.dtype), pltpu...  39.8 us
    pallas_call x1, Pallas kernels, per_device(): pl.pallas_call(place_out, out_shape=(big, big, small), in_specs=[vmem] *...  4.52 us

profile of v4, /device:TPU:1, one launch (start us, length us, event | category | flops | bytes accessed | tf_op | source)
XLA Modules:
  0.0 45.0 jit_solution(12249562413613762159)
XLA Ops:
  0.6 39.8 %shard_map.49 = (f32[14,768,128]{2,1,0:T(8,128)S(1)}, f32[14,768,128]{2,1,0:T(8,128)S(1)}, bf16[5,6,16,1024]{3,2,1,0:T(8,128)(2,1)S(1)}) custom-call(f32[14,768,128]{2,1,0:T(8,128)} %bitcast.4, f32[14,768,128]{2,1,0:T(8,128)} %bitcast.5), custom_call_target="tpu_custom_call" | custom-call | tf_op jit(solution)/shard_map/pallas_call | solution.py:542
  40.5 4.5 %shard_map.50 = (f32[14,768,128]{2,1,0:T(8,128)}, f32[14,768,128]{2,1,0:T(8,128)}, bf16[5,6,16,1024]{3,2,1,0:T(8,128)(2,1)}) custom-call(f32[14,768,128]{2,1,0:T(8,128)S(1)} %get-tuple-element.9.f_in, f32[14,768,128]{2,1,0:T(8,128)S(1)} %get-tuple-element.10.r_in, bf16[5,6,16,1024]{3,2,1,0:T(8,128)(2,1)S(1)} %get-tuple-element.11.m_in), custom_call_target="tpu_custom_call" | custom-call | tf_op jit(solution)/shard_map/pallas_call | solution.py:592
